TPU v7x, 32 devices: a whole 2x2x4 slice. The times are simulated.
32 devices in a mesh: ctx: 8 (over z, core), fsdp: 4 (over y, x).
Axes of the slice: x: 2, y: 2, z: 4, core: 2. Of those that a mesh axis runs over, the one named last changes fastest.
Arguments:
- hidden: bfloat16 [2, 4, 512, 2048], P(None, 'fsdp', 'ctx'), may hold values from -6 to 6
- cotangent: bfloat16 [2, 4, 512, 2048], P(None, 'fsdp', 'ctx'), may hold values from -6 to 6
- lengths: int32 [2, 4], P(None, 'fsdp'), may hold values from 128 to 512, as said below
- norm_gain: float32 [2048], replicated, may hold values from 0.5 to 1.5
- input_weight: bfloat16 [2048, 8512], P('fsdp'), may hold values from -0.125 to 0.125
- conv_w: float32 [4, 4352], replicated, may hold values from -3 to 3
- conv_b: float32 [4352], replicated, may hold values from -3 to 3
- dt_bias: float32 [64], replicated, may hold values from -4 to -2
- a_log: float32 [64], replicated, may hold values from -10 to -0.5
- d_skip: float32 [64], replicated, may hold values from 0.5 to 1.5
- gate_gain: float32 [4096], replicated, may hold values from 0.5 to 1.5
- output_weight: bfloat16 [4096, 2048], P('fsdp'), may hold values from -0.09375 to 0.09375
Outputs:
- out: bfloat16 [2, 4, 512, 2048], P(None, 'fsdp', 'ctx')
- d_hidden: float32 [2, 4, 512, 2048], P(None, 'fsdp', 'ctx')
- grad_norm_gain: float32 [2048], replicated
- grad_in_w: float32 [2048, 8512], P(('ctx', 'fsdp'))
- grad_conv_w: float32 [4, 4352], replicated
- grad_conv_b: float32 [4352], replicated
- grad_dt_bias: float32 [64], replicated
- grad_a_log: float32 [64], replicated
- grad_d_skip: float32 [64], replicated
- grad_gate_gain: float32 [4096], replicated
- grad_out_w: float32 [4096, 2048], P(('ctx', 'fsdp'))
Inputs may be any that keep to these rules, and one draw needn't show every extreme that they name: `lengths`: some sequence has all 512 slots live in every draw.
All inputs are finite; a program needn't handle non-finite values.
Results may differ from a plain program's by a relative error of at most 0.012.
The roundings to bfloat16 on the way count: a program that leaves them out, or rounds other values in their place, can miss the bound.
Values may be sent and summed in bfloat16 or wider, within the bound.
A program may use at most 384 MiB of HBM per device.

v0:
```python
import jax
import jax.numpy as jnp
from jax import lax
from jax.sharding import PartitionSpec as P

D = 2048
HEADS = 64
HEAD_DIM = 64
N_STATE = 128
CONV_K = 4
DI = 4096


EPS = 1e-05
EXACT_MATMUL = lax.Precision.HIGHEST


def shifted(block, axis, distance):
    devices = range(lax.axis_size(axis))
    route = [(i - distance, i) for i in devices if i - distance in devices]
    return lax.ppermute(block, axis, route)


def prefix(shard, axis, combine, identity, reverse):
    size, position = (lax.axis_size(axis), lax.axis_index(axis))
    everything = jax.tree.map(lambda part: lax.all_gather(part, axis), shard)
    start = jax.tree.map(
        lambda part, zero: jnp.broadcast_to(jnp.asarray(zero, part.dtype), part.shape),
        shard,
        identity,
    )

    def hop(k, before):
        at = size - 1 - k if reverse else k
        reached = at > position if reverse else at < position
        new = combine(before, jax.tree.map(lambda part: part[at], everything))
        return jax.tree.map(lambda a, b: jnp.where(reached, a, b), new, before)

    return lax.fori_loop(0, size, hop, start)


def rms_scale(values, gain_vec):
    return values * lax.rsqrt(jnp.mean(values * values, axis=-1, keepdims=True) + EPS) * gain_vec


def conv_front(window, dt_raw, conv_w, conv_b, dt_bias, live_mask):
    length = dt_raw.shape[1]
    pre_act = conv_b + conv_w[0] * window[:, 0:length]
    for offset in range(1, CONV_K):
        pre_act = pre_act + conv_w[offset] * window[:, offset : offset + length]
    activated = jax.nn.silu(pre_act)
    x_seq = activated[:, :, :DI]
    b_in = activated[:, :, DI : DI + N_STATE]
    c_out = activated[:, :, DI + N_STATE :]
    step_size = jax.nn.softplus(dt_raw + dt_bias) * live_mask
    return (x_seq, b_in, c_out, step_size)


def block_log(step_size, a_log):
    return jnp.cumsum(step_size * -jnp.exp(a_log), axis=1)


def block_state(x_seq, b_in, step_size, log_decay):
    seq_rows, length = (step_size.shape[0], step_size.shape[1])
    last_log = log_decay[:, length - 1 :, :]
    weighting = jnp.exp(last_log - log_decay) * step_size
    x_heads = x_seq.reshape(seq_rows, length, HEADS, HEAD_DIM) * weighting[:, :, :, None]
    local_state = jnp.einsum("sqhp,sqn->shpn", x_heads, b_in, precision=EXACT_MATMUL)
    return (jnp.exp(last_log[:, 0, :]), local_state)


def ssd_out(x_seq, b_in, c_out, step_size, log_decay, state_in, d_skip):
    seq_rows, length = (step_size.shape[0], step_size.shape[1])
    x_heads = x_seq.reshape(seq_rows, length, HEADS, HEAD_DIM)
    gram_mat = jnp.einsum("stn,skn->stk", c_out, b_in, precision=EXACT_MATMUL)
    by_head = jnp.transpose(log_decay, (0, 2, 1))
    causal = jnp.arange(length)[:, None] >= jnp.arange(length)[None, :]
    spread = by_head[:, :, :, None] - by_head[:, :, None, :]
    kernel = jnp.where(causal, jnp.exp(jnp.where(causal, spread, 0.0)), 0.0) * gram_mat[:, None]
    inputs = x_heads * step_size[:, :, :, None]
    within = jnp.einsum("shtk,skhp->sthp", kernel, inputs, precision=EXACT_MATMUL)
    carried = (
        jnp.einsum("stn,shpn->sthp", c_out, state_in, precision=EXACT_MATMUL)
        * jnp.exp(log_decay)[:, :, :, None]
    )
    result = within + carried + d_skip[:, None] * x_heads
    return result.reshape(seq_rows, length, DI)


def gate_norm(mixed_out, gate_in, gate_gain):
    return rms_scale(mixed_out * jax.nn.silu(gate_in), gate_gain)


def combine_states(earlier, later):
    return (earlier[0] * later[0], later[0][:, :, None, None] * earlier[1] + later[1])


def local(
    hidden,
    cotangent,
    lengths,
    norm_gain,
    input_weight,
    conv_w,
    conv_b,
    dt_bias,
    a_log,
    d_skip,
    gate_gain,
    output_weight,
):
    mb_count = hidden.shape[0]
    seq_rows = hidden.shape[1]
    block_len = hidden.shape[2]
    tokens = seq_rows * block_len
    proj_cols = input_weight.shape[1]
    conv_cols = conv_w.shape[1]
    rim_len = CONV_K - 1
    anchor = lax.axis_index("ctx") * block_len
    positions = anchor + jnp.arange(block_len, dtype=jnp.int32)
    identity = (
        jnp.ones((seq_rows, HEADS), jnp.float32),
        jnp.zeros((seq_rows, HEADS, HEAD_DIM, N_STATE), jnp.float32),
    )
    contract_last = (((1,), (1,)), ((), ()))
    contract_first = (((0,), (0,)), ((), ()))
    whole_fwd = (
        lax.all_gather(input_weight, "fsdp", axis=0, tiled=True),
        lax.all_gather(output_weight, "fsdp", axis=0, tiled=True),
    )
    outputs = []
    kept_values = []
    normed_list = []
    gated_list = []
    for batch_index in range(mb_count):
        full_in, full_out = whole_fwd
        source = hidden[batch_index].astype(jnp.float32)
        normed_f, norm_pull = jax.vjp(rms_scale, source, norm_gain)
        normalized_rows = normed_f.astype(jnp.bfloat16).reshape(tokens, D)
        projected_rows = jnp.dot(normalized_rows, full_in, preferred_element_type=jnp.float32)
        projected_rows = projected_rows.astype(jnp.bfloat16).reshape(seq_rows, block_len, proj_cols)
        conv_in = projected_rows[:, :, DI : DI + conv_cols]
        before = shifted(conv_in[:, block_len - rim_len :], "ctx", 1)
        window = jnp.concatenate([before, conv_in], axis=1).astype(jnp.float32)
        live_mask = (positions[None, :] < lengths[batch_index][:, None]).astype(jnp.float32)[
            :, :, None
        ]
        dt_raw = projected_rows[:, :, DI + conv_cols :].astype(jnp.float32)
        gate_in = projected_rows[:, :, :DI].astype(jnp.float32)

        def front_local(window_f, raw_f, conv_wf, conv_bf, bias_f, alog_f):
            x_seq, b_in, c_out, step_size = conv_front(
                window_f, raw_f, conv_wf, conv_bf, bias_f, live_mask
            )
            return (x_seq, b_in, c_out, step_size, block_log(step_size, alog_f))

        front_vals, front_pull = jax.vjp(
            front_local, window, dt_raw, conv_w, conv_b, dt_bias, a_log
        )
        x_seq, b_in, c_out, step_size, log_decay = front_vals
        (block_decay, local_state), state_pull = jax.vjp(
            block_state, x_seq, b_in, step_size, log_decay
        )
        state_in = prefix((block_decay, local_state), "ctx", combine_states, identity, False)[1]
        mixed_out, ssd_pull = jax.vjp(
            ssd_out, x_seq, b_in, c_out, step_size, log_decay, state_in, d_skip
        )
        gated_f, gate_pull = jax.vjp(gate_norm, mixed_out, gate_in, gate_gain)
        gated_result = gated_f.astype(jnp.bfloat16).reshape(tokens, DI)
        branch = jnp.dot(gated_result, full_out, preferred_element_type=jnp.float32)
        outputs.append((branch.reshape(seq_rows, block_len, D) + source).astype(jnp.bfloat16))
        kept_values.append(
            (norm_pull, front_pull, state_pull, ssd_pull, gate_pull, block_decay, state_in)
        )
        normed_list.append(normalized_rows)
        gated_list.append(gated_result)
    whole_back = (
        lax.all_gather(input_weight, "fsdp", axis=0, tiled=True),
        lax.all_gather(output_weight, "fsdp", axis=0, tiled=True),
    )
    grads_hidden = []
    proj_grads = []
    top_grads = []
    small_sums = []
    for batch_index in range(mb_count):
        full_in, full_out = whole_back
        norm_pull, front_pull, state_pull, ssd_pull, gate_pull, block_decay, state_in = kept_values[
            batch_index
        ]
        grad_top = cotangent[batch_index].reshape(tokens, D)
        grad_gated = lax.dot_general(
            grad_top, full_out, contract_last, preferred_element_type=jnp.float32
        )
        grad_mixed, grad_gate_in, grad_gate_gain = gate_pull(
            grad_gated.reshape(seq_rows, block_len, DI)
        )
        grad_x, grad_b, grad_c, grad_step, grad_log, grad_carry, grad_skip = ssd_pull(grad_mixed)
        grad_out_state = prefix((block_decay, grad_carry), "ctx", combine_states, identity, True)[1]
        grad_decay = jnp.sum(grad_out_state * state_in, axis=(2, 3))
        more_x, more_b, more_step, more_log = state_pull((grad_decay, grad_out_state))
        grad_window, grad_raw, grad_conv_w, grad_conv_b, grad_bias, grad_alog = front_pull(
            (grad_x + more_x, grad_b + more_b, grad_c, grad_step + more_step, grad_log + more_log)
        )
        from_next = shifted(grad_window[:, :rim_len].astype(jnp.bfloat16), "ctx", -1).astype(
            jnp.float32
        )
        grad_conv_in = grad_window[:, rim_len:] + jnp.pad(
            from_next, ((0, 0), (block_len - rim_len, 0), (0, 0))
        )
        grad_proj = jnp.concatenate([grad_gate_in, grad_conv_in, grad_raw], axis=2).astype(
            jnp.bfloat16
        )
        grad_proj = grad_proj.reshape(tokens, proj_cols)
        grad_normed = lax.dot_general(
            grad_proj, full_in, contract_last, preferred_element_type=jnp.float32
        )
        grad_source, grad_norm_gain = norm_pull(grad_normed.reshape(seq_rows, block_len, D))
        grads_hidden.append(grad_source + cotangent[batch_index].astype(jnp.float32))
        proj_grads.append(grad_proj)
        top_grads.append(grad_top)
        terms = (
            grad_norm_gain,
            grad_conv_w,
            grad_conv_b,
            grad_bias,
            grad_alog,
            grad_skip,
            grad_gate_gain,
        )
        if batch_index == 0:
            small_sums = terms
        else:
            small_sums = jax.tree.map(jnp.add, small_sums, terms)
    normed_all = jnp.concatenate(normed_list, axis=0)
    gated_all = jnp.concatenate(gated_list, axis=0)
    proj_all = jnp.concatenate(proj_grads, axis=0)
    top_all = jnp.concatenate(top_grads, axis=0)
    normed_mine, gated_mine = (
        lax.all_to_all(normed_all, "ctx", split_axis=1, concat_axis=0, tiled=True),
        lax.all_to_all(gated_all, "ctx", split_axis=1, concat_axis=0, tiled=True),
    )
    partial_in = lax.dot_general(
        normed_mine,
        lax.all_gather(proj_all, "ctx", axis=0, tiled=True),
        contract_first,
        preferred_element_type=jnp.float32,
    )
    partial_out = lax.dot_general(
        gated_mine,
        lax.all_gather(top_all, "ctx", axis=0, tiled=True),
        contract_first,
        preferred_element_type=jnp.float32,
    )
    grad_in_w, grad_out_w = (
        lax.psum_scatter(
            partial_in.astype(jnp.bfloat16), "fsdp", scatter_dimension=0, tiled=True
        ).astype(jnp.float32),
        lax.psum_scatter(
            partial_out.astype(jnp.bfloat16), "fsdp", scatter_dimension=0, tiled=True
        ).astype(jnp.float32),
    )
    summed = lax.psum(small_sums, ("ctx", "fsdp"))
    return (
        jnp.stack(outputs),
        jnp.stack(grads_hidden),
        summed[0],
        grad_in_w,
        summed[1],
        summed[2],
        summed[3],
        summed[4],
        summed[5],
        summed[6],
        grad_out_w,
    )


def solution(mesh):
    in_specs = (
        P(None, "fsdp", "ctx", None),
        P(None, "fsdp", "ctx", None),
        P(None, "fsdp"),
        P(),
        P("fsdp", None),
        P(),
        P(),
        P(),
        P(),
        P(),
        P(),
        P("fsdp", None),
    )
    out_specs = (
        P(None, "fsdp", "ctx", None),
        P(None, "fsdp", "ctx", None),
        P(),
        P(("ctx", "fsdp"), None),
        P(),
        P(),
        P(),
        P(),
        P(),
        P(),
        P(("ctx", "fsdp"), None),
    )
    return jax.shard_map(local, mesh=mesh, in_specs=in_specs, out_specs=out_specs, check_vma=False)
```

profile of v0, /device:TPU:1, one launch (start us, length us, event | category | flops | bytes accessed | tf_op | source)
XLA Modules:
  0.0 1669.9 jit_solution(16836983003102642011)
XLA Ops:
  11.8 309.3 %all-gather.13.cloned.1.call-done = bf16[2048,8512]{0,1:T(8,128)(2,1)} async-done(((bf16[512,8512]{0,1:T(8,128)(2,1)}), bf16[2048,8512]{0,1:T(8,128)(2,1)}) %all-gather.13.cloned.1.call-update) | async-done | bytes 34865168 | tf_op jit(solution)/shard_map/all_gather | solution.py:128
  321.1 17.8 %fusion.4 = bf16[1,64,8512]{2,1,0:T(8,128)(2,1)S(1)} fusion(bf16[2048,8512]{0,1:T(8,128)(2,1)} %all-gather.13.cloned.1.call-done, f32[2048]{0:T(1024)S(1)} %copy-done.45, f32[64]{0:T(128)S(1)} %fusion.250, bf16[2,1,64,2048]{3,2,1,0:T(8,128)(2,1)S(1)} %copy-done.22), kind=kOutput, calls=%fused_computation.15 | convolution fusion | flops 2232438784 | bytes 36225536 | tf_op jit(solution)/shard_map/dot_general | solution.py:140
  339.9 15.5 fusion.5
  399.8 80.6 %all-gather.15.cloned.1.call-done = bf16[4096,2048]{1,0:T(8,128)(2,1)} async-done(((bf16[1024,2048]{1,0:T(8,128)(2,1)}), bf16[4096,2048]{1,0:T(8,128)(2,1)}) %all-gather.15.cloned.1.call-update) | async-done | bytes 16777232 | tf_op jit(solution)/shard_map/all_gather | solution.py:129
  480.4 12.0 fusion.261
  500.3 13.0 all_gather.55
  513.3 18.6 %all_gather.51 = f32[8,1,64]{2,1,0:T(1,128)} all-gather(f32[1,1,64]{2,1,0:T(1,128)} %get-tuple-element.775), channel_id=1, replica_groups=mesh['ctx'=8,'fsdp'=4] {'ctx'}, dimensions={0}, use_global_device_ids=true | all-gather | bytes 2304 | tf_op jit(solution)/shard_map/all_gather | solution.py:26
  547.0 86.6 %all-gather.23.cloned.1.call-done = f32[512,64,128]{2,1,0:T(8,128)} async-done(((f32[64,64,128]{2,1,0:T(8,128)}), f32[512,64,128]{2,1,0:T(8,128)}) %all-gather.23.cloned.1.call-update) | async-done | bytes 16777232 | tf_op jit(solution)/shard_map/all_gather | solution.py:26
  633.6 40.7 %while.61 = (s32[]{:T(128)}, f32[1,64,64,128]{3,2,1,0:T(8,128)}, s32[]{:T(128)}, f32[8,1,64]{2,1,0:T(1,128)}, f32[8,1,64,64,128]{4,3,2,1,0:T(8,128)}, /*index=5*/s32[]{:T(128)}, s32[]{:T(128)}) while((s32[]{:T(128)}, f32[1,64,64,128]{3,2,1,0:T(8,128)}, s32[]{:T(128)}, f32[8,1,64]{2,1,0:T(1,128)}, ...), condition=%wide.region_8.10_spmd.clone, body=%wide.region_7.9_spmd.clone.sunk | while | flops 2097156 | bytes 6292337 | solution.py:39
  693.0 91.4 %all-gather.21.cloned.1.call-done = f32[512,64,128]{2,1,0:T(8,128)} async-done(((f32[64,64,128]{2,1,0:T(8,128)}), f32[512,64,128]{2,1,0:T(8,128)}) %all-gather.21.cloned.1.call-update) | async-done | bytes 16777232 | tf_op jit(solution)/shard_map/all_gather | solution.py:26
  784.4 25.9 %while.60 = (s32[]{:T(128)}, f32[1,64,64,128]{3,2,1,0:T(8,128)S(1)}, s32[]{:T(128)}, f32[8,1,64]{2,1,0:T(1,128)}, f32[8,1,64,64,128]{4,3,2,1,0:T(8,128)}, /*index=5*/s32[]{:T(128)}, s32[]{:T(128)}) while((s32[]{:T(128)}, f32[1,64,64,128]{3,2,1,0:T(8,128)S(1)}, s32[]{:T(128)}, f32[8,1,64]{2,1,0:T(1,128)}, ...), condition=%wide.region_3.5_spmd.clone, body=%wide.region_2.4_spmd.clone.sunk | while | flops 2097156 | bytes 6292337 | solution.py:39
  829.1 13.8 fusion.129
  958.5 52.2 %all-gather.25.cloned.1.call-done = f32[512,64,128]{2,1,0:T(8,128)} async-done(((f32[64,64,128]{2,1,0:T(8,128)}), f32[512,64,128]{2,1,0:T(8,128)}) %all-gather.25.cloned.1.call-update) | async-done | bytes 16777232 | tf_op jit(solution)/shard_map/all_gather | solution.py:26
  1010.7 37.1 %while.62 = (s32[]{:T(128)}, f32[1,64,64,128]{3,2,1,0:T(8,128)}, s32[]{:T(128)}, f32[8,1,64]{2,1,0:T(1,128)}, f32[8,1,64,64,128]{4,3,2,1,0:T(8,128)}, /*index=5*/s32[]{:T(128)}, s32[]{:T(128)}, s32[]{:T(128)}, s32[]{:T(128)}) while((s32[]{:T(128)}, f32[1,64,64,128]{3,2,1,0:T(8,128)}, s32[]{:T(128)}, f32[8,1,64]{2,1,0:T(1,128)}, ...), condition=%wide.region_13.15_spmd.clone, body=%wide.region_12.14_spmd.clone.sunk | while | flops 2097160 | bytes 6292399 | solution.py:39
  1056.7 104.9 %all-gather.27.cloned.1.call-done = f32[512,64,128]{2,1,0:T(8,128)} async-done(((f32[64,64,128]{2,1,0:T(8,128)}), f32[512,64,128]{2,1,0:T(8,128)}) %all-gather.27.cloned.1.call-update) | async-done | bytes 16777232 | tf_op jit(solution)/shard_map/all_gather | solution.py:26
  1161.6 36.6 %while.63 = (s32[]{:T(128)}, f32[1,64,64,128]{3,2,1,0:T(8,128)}, s32[]{:T(128)}, f32[8,1,64]{2,1,0:T(1,128)}, f32[8,1,64,64,128]{4,3,2,1,0:T(8,128)}, /*index=5*/s32[]{:T(128)}, s32[]{:T(128)}, s32[]{:T(128)}, s32[]{:T(128)}) while((s32[]{:T(128)}, f32[1,64,64,128]{3,2,1,0:T(8,128)}, s32[]{:T(128)}, f32[8,1,64]{2,1,0:T(1,128)}, ...), condition=%wide.region_26.28_spmd.clone, body=%wide.region_25.27_spmd.clone.sunk | while | flops 2097160 | bytes 6292399 | solution.py:39
  1261.8 50.1 %all-to-all-done.1 = bf16[128,8,512]{2,0,1:T(8,128)(2,1)} async-done(((bf16[128,8,512]{2,0,1:T(8,128)(2,1)}), bf16[128,8,512]{2,0,1:T(8,128)(2,1)}, u32[]{:S(2)}, u32[]{:S(2)}) %all-to-all-start.1) | async-done | bytes 1048608 | tf_op jit(solution)/shard_map/all_to_all | solution.py:240
  1320.0 37.1 %all_to_all.32 = bf16[128,8,256]{2,0,1:T(8,128)(2,1)} all-to-all(bf16[128,8,256]{2,0,1:T(8,128)(2,1)S(1)} %pad_maximum_fusion.3), channel_id=1, replica_groups=mesh['ctx'=8,'fsdp'=4] {'ctx'}, dimensions={1} | all-to-all | bytes 1048576 | tf_op jit(solution)/shard_map/all_to_all | solution.py:239
  1357.1 83.6 %all-gather.17.cloned.1.call-done = bf16[1024,8512]{1,0:T(8,128)(2,1)} async-done(((bf16[128,8512]{1,0:T(8,128)(2,1)}), bf16[1024,8512]{1,0:T(8,128)(2,1)}) %all-gather.17.cloned.1.call-update) | async-done | bytes 17432592 | tf_op jit(solution)/shard_map/all_gather | solution.py:244
  1440.7 13.0 convolution_convert_fusion
  1480.6 14.8 fusion.110
  1495.5 15.3 fusion.173
  1512.3 40.1 %all-reduce.26 = (f32[2048]{0:T(1024)}, f32[4352]{0:T(1024)}, f32[64]{0:T(128)}, f32[64]{0:T(128)}, f32[64]{0:T(128)}, /*index=5*/f32[4096]{0:T(1024)}) all-reduce(f32[2048]{0:T(1024)S(1)} %add.491, f32[4352]{0:T(1024)S(1)} %add.493, f32[64]{0:T(128)S(1)} %add.494, ...), channel_id=1, replica_groups=mesh['ctx'=8,'fsdp'=4] {'ctx','fsdp'}, use_global_device_ids=true, to_apply=%region_38.40 | all-reduce | flops 10688 | bytes 85504 | tf_op jit(solution)/shard_map/psum | solution.py:262
  1555.1 106.5 %all-reduce.29.cloned.1.call-done = f32[4,4352]{1,0:T(4,128)} async-done(((f32[4,4352]{1,0:T(4,128)}), f32[4,4352]{1,0:T(4,128)}) %all-reduce.29.cloned.1.call-update) | async-done | bytes 69648 | tf_op jit(solution)/shard_map/psum | solution.py:262
  (538 shorter events, 477.4 us)
Async XLA Ops:
  7.2 313.9 %all-gather.13.cloned.1.call-start = ((), (), s32[]{:S(2)}) async-start(), calls=%async_computation.4 | async-start | bytes 43581440 | tf_op jit(solution)/shard_map/all_gather | solution.py:128
  8.0 472.4 %all-gather.15.cloned.1.call-start = ((), (), s32[]{:S(2)}) async-start(), calls=%async_computation.5 | async-start | bytes 20971520 | tf_op jit(solution)/shard_map/all_gather | solution.py:129
  8.7 624.9 %all-gather.23.cloned.1.call-start = ((), (), s32[]{:S(2)}) async-start(), calls=%async_computation.12 | async-start | bytes 18874368 | tf_op jit(solution)/shard_map/all_gather | solution.py:26
  10.0 353.3 %copy-start.104 = (f32[64]{0:T(128)}, f32[64]{0:T(128)S(1)}, u32[]{:S(2)}) copy-start(f32[64]{0:T(128)S(1)} %compare_convert_fusion) | copy-start | bytes 772
  10.7 371.2 %copy-start.107 = (f32[64]{0:T(128)}, f32[64]{0:T(128)S(1)}, u32[]{:S(2)}) copy-start(f32[64]{0:T(128)S(1)} %compare_convert_fusion.1) | copy-start | bytes 772
  10.9 357.0 %copy-start.55 = (f32[4352]{0:T(1024)}, f32[4352]{0:T(1024)S(1)}, u32[]{:S(2)}) copy-start(f32[4352]{0:T(1024)S(1)} %get-tuple-element.659) | copy-start | bytes 52228
  10.9 357.0 %copy-start.57 = (f32[4352]{0:T(1024)}, f32[4352]{0:T(1024)S(1)}, u32[]{:S(2)}) copy-start(f32[4352]{0:T(1024)S(1)} %get-tuple-element.660) | copy-start | bytes 52228
  10.9 357.0 %copy-start.59 = (f32[4352]{0:T(1024)}, f32[4352]{0:T(1024)S(1)}, u32[]{:S(2)}) copy-start(f32[4352]{0:T(1024)S(1)} %get-tuple-element.661) | copy-start | bytes 52228
  10.9 357.0 %copy-start.61 = (f32[4352]{0:T(1024)}, f32[4352]{0:T(1024)S(1)}, u32[]{:S(2)}) copy-start(f32[4352]{0:T(1024)S(1)} %get-tuple-element.662) | copy-start | bytes 52228
  11.8 328.1 %copy-start.102 = (f32[64]{0:T(128)}, f32[64]{0:T(128)S(1)}, u32[]{:S(2)}) copy-start(f32[64]{0:T(128)S(1)} %fusion.252) | copy-start | bytes 772
  11.8 350.2 %copy-start.123 = (f32[64]{0:T(128)}, f32[64]{0:T(128)S(1)}, u32[]{:S(2)}) copy-start(f32[64]{0:T(128)S(1)} %exponential_negate_fusion) | copy-start | bytes 772
  356.1 9.6 collective-permute-start
  359.9 7.1 collective-permute-start.1
  380.5 403.9 %all-gather.21.cloned.1.call-start = ((), (), s32[]{:S(2)}) async-start(), calls=%async_computation.11 | async-start | bytes 18874368 | tf_op jit(solution)/shard_map/all_gather | solution.py:26
  399.1 611.6 %all-gather.25.cloned.1.call-start = ((), (), s32[]{:S(2)}) async-start(), calls=%async_computation.13 | async-start | bytes 18874368 | tf_op jit(solution)/shard_map/all_gather | solution.py:26
  861.2 300.3 %all-gather.27.cloned.1.call-start = ((), (), s32[]{:S(2)}) async-start(), calls=%async_computation.14 | async-start | bytes 18874368 | tf_op jit(solution)/shard_map/all_gather | solution.py:26
  877.6 384.1 %all-gather.19.cloned.1.call-start = ((), (), s32[]{:S(2)}) async-start(), calls=%async_computation.9 | async-start | bytes 4718592 | tf_op jit(solution)/shard_map/all_gather | solution.py:250
  879.7 561.0 %all-gather.17.cloned.1.call-start = ((), (), s32[]{:S(2)}) async-start(), calls=%async_computation.6 | async-start | bytes 19759104 | tf_op jit(solution)/shard_map/all_gather | solution.py:244
  1235.3 6.7 collective-permute-start.3
  1238.5 5.4 collective-permute-start.2
  1257.5 54.4 %all-to-all-start.1 = ((bf16[128,8,512]{2,0,1:T(8,128)(2,1)}), bf16[128,8,512]{2,0,1:T(8,128)(2,1)}, u32[]{:S(2)}, u32[]{:S(2)}) async-start(bf16[128,8,512]{2,0,1:T(8,128)(2,1)} %pad_maximum_fusion.1), calls=%async_computation.2 | async-start | bytes 2097152 | tf_op jit(solution)/shard_map/all_to_all | solution.py:240
  1261.7 215.7 %reduce-scatter.5.cloned.1.call-start = ((), (), s32[]{:S(2)}) async-start(), calls=%async_computation.10 | async-start | bytes 2621440 | tf_op jit(solution)/shard_map/reduce_scatter | solution.py:258
  1318.1 234.2 %reduce-scatter.3.cloned.1.call-start = ((), (), s32[]{:S(2)}) async-start(), calls=%async_computation.7 | async-start | bytes 5488640 | tf_op jit(solution)/shard_map/reduce_scatter | solution.py:255
  1453.8 207.9 %all-reduce.29.cloned.1.call-start = ((), (), s32[]{:S(2)}) async-start(), calls=%async_computation.8 | async-start | bytes 139264 | tf_op jit(solution)/shard_map/psum | solution.py:262
  (128 other events, 1330.1 us)
Sparse Core Ops, SparseCore 0:
  9.9 311.1 all-gather.12
  322.9 157.4 all-gather.14
  482.0 151.5 all-gather.22
  635.1 149.2 all-gather.20
  861.4 149.3 all-gather.24
  1012.2 149.3 all-gather.26
  1163.2 45.3 all-gather.18
  1254.8 185.8 all-gather.16
  1443.7 33.6 reduce-scatter.4
  1480.5 54.6 reduce-scatter.2
  1542.4 119.1 all-reduce.28
where the time goes:
time: 1680 us; the launch traced here: 1670 us
  waiting for transfers between devices  971 us (58%)
  matrix products  239 us (14%)
  other arithmetic  190 us (11%)
  local copies, waits for them, and re-layouts  129 us (8%)
  blocking collectives  109 us (6%)
    all_gather x4, waiting for transfers between devices, prefix(): everything = jax.tree.map(lambda part: lax.all_gather(part, axis), shard)  335 us
    all_gather x1, waiting for transfers between devices, local(): lax.all_gather(input_weight, 'fsdp', axis=0, tiled=True)  309 us
    select_n x32, other arithmetic, hop(): return jax.tree.map(lambda a, b: jnp.where(reached, a, b), new, before)  112 us
    psum x1, waiting for transfers between devices, local(): summed = lax.psum(small_sums, ('ctx', 'fsdp'))  107 us
    all_gather x1, waiting for transfers between devices, local(): lax.all_gather(proj_all, 'ctx', axis=0, tiled=True)  83.6 us
    all_gather x1, waiting for transfers between devices, local(): lax.all_gather(output_weight, 'fsdp', axis=0, tiled=True)  80.6 us
    all_to_all x1, waiting for transfers between devices, local(): lax.all_to_all(gated_all, 'ctx', split_axis=1, concat_axis=0, tiled=True)  50.1 us
    dot_general x6, matrix products, ssd_out(): jnp.einsum('shtk,skhp->sthp', kernel, inputs, precision=EXACT_MATMUL)  44 us
  transfers between devices with their start and end apart: 16, of which 11 were waited for; matrix products, arithmetic and copies ran while one was open for 29% of the time, Pallas kernels for 0%

commit v1 on v0

v1 whole, which is shorter than its diff:
```python
import functools

import jax
import jax.numpy as jnp
from jax import lax
from jax.experimental import pallas as pl
from jax.experimental.pallas import tpu as pltpu
from jax.sharding import PartitionSpec as P

D = 2048
HEADS = 64
HEAD_DIM = 64
N_STATE = 128
CONV_K = 4
DI = 4096
CH = DI + 2 * N_STATE
LANES = 128
EPS = 1e-05
F32 = jnp.float32
BF16 = jnp.bfloat16
EXACT = lax.Precision.HIGHEST
VMEM_LIMIT = 60 * 1024 * 1024


def dot(a, b, ca=1, cb=0):
    return lax.dot_general(
        a.astype(BF16), b.astype(BF16), (((ca,), (cb,)), ((), ())), preferred_element_type=F32
    )


def dot_exact(a, b):
    return lax.dot_general(
        a, b, (((1,), (0,)), ((), ())), precision=EXACT, preferred_element_type=F32
    )


def to_lanes(per_head, width):
    q = per_head.shape[0]
    low = lax.broadcasted_iota(jnp.int32, (q, LANES), 1) < HEAD_DIM
    pairs = []
    for j in range(width // LANES):
        first = jnp.broadcast_to(per_head[:, 2 * j : 2 * j + 1], (q, LANES))
        second = jnp.broadcast_to(per_head[:, 2 * j + 1 : 2 * j + 2], (q, LANES))
        pairs.append(jnp.where(low, first, second))
    return jnp.concatenate(pairs, axis=1)


def head_sum_matrix(width):
    channel = lax.broadcasted_iota(jnp.int32, (width, LANES), 0) // HEAD_DIM
    return (channel == lax.broadcasted_iota(jnp.int32, (width, LANES), 1)).astype(F32)


def split_heads(pair):
    low = lax.broadcasted_iota(jnp.int32, pair.shape, 1) < HEAD_DIM
    zero = jnp.zeros_like(pair)
    return jnp.concatenate([jnp.where(low, pair, zero), jnp.where(low, zero, pair)], axis=0)


def triangle(q, lower):
    rows = lax.broadcasted_iota(jnp.int32, (q, q), 0)
    cols = lax.broadcasted_iota(jnp.int32, (q, q), 1)
    return (rows >= cols) if lower else (rows <= cols)


def softplus(z):
    return jnp.maximum(z, 0.0) + jnp.log(1.0 + jnp.exp(-jnp.abs(z)))


def live_column(lengths_ref, s, chunk, q):
    slots = chunk * q + lax.broadcasted_iota(jnp.int32, (q, LANES), 0)
    return (slots < lengths_ref[s]).astype(F32)


def decays(dt_raw, bias, rate, live):
    q = dt_raw.shape[0]
    z = dt_raw + bias
    step = softplus(z) * live
    cum = dot_exact(triangle(q, True).astype(F32), step * rate)
    return z, step, cum


def forward_kernel(
    cw, lengths, proj, conv_w, heads_par, chan_par, grad_gated, mixed_out, pre_out, state_out,
    stats_out, window, state,
):
    chunk = pl.program_id(0)
    seqs = proj.shape[1]
    q = proj.shape[0] * proj.shape[2]
    cc = cw + 2 * N_STATE
    causal = triangle(q, True)

    @pl.when(chunk == 0)
    def _():
        window[...] = jnp.zeros_like(window)
        state[...] = jnp.zeros_like(state)

    for s in range(seqs):
        rows = proj[:, s].reshape(q, proj.shape[3])
        gate = rows[:, :cw].astype(F32)
        window[s, 8 : 8 + q, :] = rows[:, cw : cw + cc].astype(F32)
        pre = conv_w[CONV_K : CONV_K + 1, :] + conv_w[0:1, :] * window[s, 5 : 5 + q, :]
        for k in range(1, CONV_K):
            pre = pre + conv_w[k : k + 1, :] * window[s, 5 + k : 5 + k + q, :]
        window[s, 0:8, :] = window[s, q : q + 8, :]
        pre_out[0, s] = pre
        act = pre * jax.nn.sigmoid(pre)
        x = act[:, :cw]
        b = act[:, cw : cw + N_STATE]
        c = act[:, cw + N_STATE :]
        live = live_column(lengths, s, chunk, q)
        _, step, cum = decays(
            rows[:, cw + cc :].astype(F32), heads_par[0:1, :], heads_par[1:2, :], live
        )
        cum_t = cum.T
        last = cum[q - 1 : q, :]
        u = x * to_lanes(step, cw)
        gram = dot(c, b, 1, 1)
        within = []
        for j in range(cw // LANES):
            kernels = []
            for h in (2 * j, 2 * j + 1):
                spread = jnp.where(causal, cum[:, h : h + 1] - cum_t[h : h + 1, :], -1e30)
                kernels.append((gram * jnp.exp(spread)).astype(BF16))
            both = jnp.concatenate(kernels, axis=1)
            within.append(dot(both, split_heads(u[:, j * LANES : (j + 1) * LANES])))
        before = state[s]
        state_out[0, s] = before
        mixed = (
            jnp.concatenate(within, axis=1)
            + dot(c, before) * to_lanes(jnp.exp(cum), cw)
            + chan_par[0:1, :] * x
        )
        mixed_out[0, s] = mixed
        left = to_lanes(jnp.exp(last - cum), cw)
        state[s] = before * to_lanes(jnp.exp(last), cw) + dot(b, left * u, 0, 0)
        g = mixed * gate * jax.nn.sigmoid(gate)
        gg = grad_gated[:, s].reshape(q, cw)
        ones = jnp.ones((8, cw), F32)
        first = lax.dot_general(
            ones, g * g, (((1,), (1,)), ((), ())), precision=EXACT, preferred_element_type=F32
        )
        second = lax.dot_general(
            ones, gg * chan_par[1:2, :] * g, (((1,), (1,)), ((), ())), precision=EXACT,
            preferred_element_type=F32,
        )
        stats_out[0, s, 0:1, :] = first[0:1, :]
        stats_out[0, s, 1:2, :] = second[0:1, :]


def backward_kernel(
    cw, chunks, lengths, proj, conv_w, heads_par, chan_par, grad_gated, mixed_in, pre_in, state_in,
    scale_in, dproj_out, dconv_out, dheads_out, dchan_out, window, state_grad,
):
    step_id = pl.program_id(0)
    chunk = chunks - 1 - step_id
    seqs = proj.shape[1]
    q = proj.shape[0] * proj.shape[2]
    blocks = proj.shape[0]
    cc = cw + 2 * N_STATE
    causal = triangle(q, True)
    sums = head_sum_matrix(cw)

    @pl.when(step_id == 0)
    def _():
        window[...] = jnp.zeros_like(window)
        state_grad[...] = jnp.zeros_like(state_grad)
        dconv_out[...] = jnp.zeros_like(dconv_out)
        dheads_out[...] = jnp.zeros_like(dheads_out)
        dchan_out[...] = jnp.zeros_like(dchan_out)

    for s in range(seqs):
        rows = proj[:, s].reshape(q, proj.shape[3])
        gate = rows[:, :cw].astype(F32)
        conv_in = rows[:, cw : cw + cc].astype(F32)
        pre = pre_in[0, s]
        mixed = mixed_in[0, s]
        gg = grad_gated[:, s].reshape(q, cw)
        scale = jnp.concatenate(
            [jnp.broadcast_to(scale_in[0, s, 0:1, :], (LANES, q)).T] * (cw // LANES), axis=1
        )
        pull = jnp.concatenate(
            [jnp.broadcast_to(scale_in[0, s, 1:2, :], (LANES, q)).T] * (cw // LANES), axis=1
        )
        sig = jax.nn.sigmoid(gate)
        silu = gate * sig
        g = mixed * silu
        dchan_out[1:2, :] += jnp.sum(gg * g * scale, axis=0, keepdims=True)
        dg = scale * (gg * chan_par[1:2, :] - g * pull)
        gm = dg * silu
        dgate = dg * mixed * (sig * (1.0 + gate * (1.0 - sig)))
        sig_pre = jax.nn.sigmoid(pre)
        act = pre * sig_pre
        x = act[:, :cw]
        b = act[:, cw : cw + N_STATE]
        c = act[:, cw + N_STATE :]
        live = live_column(lengths, s, chunk, q)
        z, step, cum = decays(
            rows[:, cw + cc :].astype(F32), heads_par[0:1, :], heads_par[1:2, :], live
        )
        cum_t = cum.T
        last = cum[q - 1 : q, :]
        step_l = to_lanes(step, cw)
        u = x * step_l
        gram = dot(c, b, 1, 1)
        dchan_out[0:1, :] += jnp.sum(gm * x, axis=0, keepdims=True)
        du = []
        dgram = jnp.zeros((q, q), F32)
        for j in range(cw // LANES):
            at = slice(j * LANES, (j + 1) * LANES)
            dkernels = dot(gm[:, at], split_heads(u[:, at]), 1, 1)
            kernels = []
            for i in range(2):
                h = 2 * j + i
                spread = jnp.where(causal, cum[:, h : h + 1] - cum_t[h : h + 1, :], -1e30)
                decay = jnp.exp(spread)
                dgram = dgram + dkernels[:, i * q : (i + 1) * q] * decay
                kernels.append((gram * decay).astype(BF16))
            both = jnp.concatenate(kernels, axis=0)
            du.append(dot(both, split_heads(gm[:, at]), 0, 0))
        before = state_in[0, s]
        after_grad = state_grad[s]
        v = gm * to_lanes(jnp.exp(cum), cw)
        left = to_lanes(jnp.exp(last - cum), cw)
        du_state = left * dot(b, after_grad)
        du = jnp.concatenate(du, axis=1) + du_state
        dc = dot(dgram, b) + dot(v, before, 1, 1)
        db = dot(dgram, c, 0, 0) + dot(left * u, after_grad, 1, 1)
        end = to_lanes(jnp.exp(last), cw)
        extra = jnp.sum(u * du_state, axis=0, keepdims=True) + end * jnp.sum(
            after_grad * before, axis=0, keepdims=True
        )
        state_grad[s] = end * after_grad + dot(c, v, 0, 0)
        last_row = (lax.broadcasted_iota(jnp.int32, (q, LANES), 0) == q - 1).astype(F32)
        dcum = dot_exact(gm * (mixed - chan_par[0:1, :] * x) - u * du, sums) + last_row * dot_exact(
            jnp.broadcast_to(extra, (8, cw)), sums
        )[0:1, :]
        dlog = dot_exact(triangle(q, False).astype(F32), dcum)
        rate = heads_par[1:2, :]
        dstep = dot_exact(x * du, sums) + dlog * rate
        dheads_out[1:2, :] += jnp.sum(dlog * step * rate, axis=0, keepdims=True)
        dz = dstep * live * jax.nn.sigmoid(z)
        dheads_out[0:1, :] += jnp.sum(dz, axis=0, keepdims=True)
        dx = step_l * du + chan_par[0:1, :] * gm
        dpre = jnp.concatenate([dx, db, dc], axis=1) * (sig_pre * (1.0 + pre * (1.0 - sig_pre)))
        window[s, 0:q, :] = dpre
        dconv_in = jnp.zeros((q, cc), F32)
        for k in range(CONV_K):
            ahead = CONV_K - 1 - k
            moved = window[s, ahead : ahead + q, :]
            dconv_in = dconv_in + conv_w[k : k + 1, :] * moved
            dconv_out[k : k + 1, :] += jnp.sum(conv_in * moved, axis=0, keepdims=True)
        dconv_out[CONV_K : CONV_K + 1, :] += jnp.sum(dpre, axis=0, keepdims=True)
        window[s, q : q + 8, :] = window[s, 0:8, :]
        dproj_out[:, s, :, :cw] = dgate.astype(BF16).reshape(blocks, q // blocks, cw)
        dproj_out[:, s, :, cw : cw + cc] = dconv_in.astype(BF16).reshape(blocks, q // blocks, cc)
        dproj_out[:, s, :, cw + cc :] = dz.astype(BF16).reshape(blocks, q // blocks, LANES)


def call_forward(cw, per, lengths, proj, conv_w, heads_par, chan_par, grad_gated):
    nc, seqs, length, cols = proj.shape
    chunks, q, cc = nc // per, per * length, cw + 2 * N_STATE
    whole = lambda a: pl.BlockSpec(a.shape, lambda i: (0,) * a.ndim)
    by_chunk = lambda n: pl.BlockSpec((1, seqs, n[0], n[1]), lambda i: (i, 0, 0, 0))
    tokens = lambda n: pl.BlockSpec((per, seqs, length, n), lambda i: (i, 0, 0, 0))
    return pl.pallas_call(
        functools.partial(forward_kernel, cw),
        grid=(chunks,),
        in_specs=[
            pl.BlockSpec(memory_space=pltpu.SMEM),
            tokens(cols),
            whole(conv_w),
            whole(heads_par),
            whole(chan_par),
            tokens(cw),
        ],
        out_specs=[
            by_chunk((q, cw)),
            by_chunk((q, cc)),
            by_chunk((N_STATE, cw)),
            by_chunk((8, q)),
        ],
        out_shape=[
            jax.ShapeDtypeStruct((chunks, seqs, q, cw), F32),
            jax.ShapeDtypeStruct((chunks, seqs, q, cc), F32),
            jax.ShapeDtypeStruct((chunks, seqs, N_STATE, cw), F32),
            jax.ShapeDtypeStruct((chunks, seqs, 8, q), F32),
        ],
        scratch_shapes=[
            pltpu.VMEM((seqs, q + 8, cc), F32),
            pltpu.VMEM((seqs, N_STATE, cw), F32),
        ],
        compiler_params=pltpu.CompilerParams(vmem_limit_bytes=VMEM_LIMIT),
        name="mixer_forward",
    )(lengths, proj, conv_w, heads_par, chan_par, grad_gated)


def call_backward(
    cw, per, lengths, proj, conv_w, heads_par, chan_par, grad_gated, mixed, pre, states, scales
):
    nc, seqs, length, cols = proj.shape
    chunks, q, cc = nc // per, per * length, cw + 2 * N_STATE
    whole = lambda shape: pl.BlockSpec(shape, lambda i: (0,) * len(shape))
    by_chunk = lambda n: pl.BlockSpec((1, seqs, n[0], n[1]), lambda i: (chunks - 1 - i, 0, 0, 0))
    tokens = lambda n: pl.BlockSpec(
        (per, seqs, length, n), lambda i: (chunks - 1 - i, 0, 0, 0)
    )
    return pl.pallas_call(
        functools.partial(backward_kernel, cw, chunks),
        grid=(chunks,),
        in_specs=[
            pl.BlockSpec(memory_space=pltpu.SMEM),
            tokens(cols),
            whole(conv_w.shape),
            whole(heads_par.shape),
            whole(chan_par.shape),
            tokens(cw),
            by_chunk((q, cw)),
            by_chunk((q, cc)),
            by_chunk((N_STATE, cw)),
            by_chunk((8, q)),
        ],
        out_specs=[
            tokens(cols),
            whole((8, cc)),
            whole((8, LANES)),
            whole((8, cw)),
        ],
        out_shape=[
            jax.ShapeDtypeStruct(proj.shape, BF16),
            jax.ShapeDtypeStruct((8, cc), F32),
            jax.ShapeDtypeStruct((8, LANES), F32),
            jax.ShapeDtypeStruct((8, cw), F32),
        ],
        scratch_shapes=[
            pltpu.VMEM((seqs, q + 8, cc), F32),
            pltpu.VMEM((seqs, N_STATE, cw), F32),
        ],
        compiler_params=pltpu.CompilerParams(vmem_limit_bytes=VMEM_LIMIT),
        name="mixer_backward",
    )(lengths, proj, conv_w, heads_par, chan_par, grad_gated, mixed, pre, states, scales)


def rms_scale(values, gain_vec):
    return values * lax.rsqrt(jnp.mean(values * values, axis=-1, keepdims=True) + EPS) * gain_vec


def local(
    hidden,
    cotangent,
    lengths,
    norm_gain,
    input_weight,
    conv_w,
    conv_b,
    dt_bias,
    a_log,
    d_skip,
    gate_gain,
    output_weight,
):
    nc, nf = lax.axis_size("ctx"), lax.axis_size("fsdp")
    me_c, me_f = lax.axis_index("ctx"), lax.axis_index("fsdp")
    mb_count, seq_rows, length = hidden.shape[0], hidden.shape[1], hidden.shape[2]
    seqs = mb_count * seq_rows
    mine = seqs * length
    heads = HEADS // nc
    cw = DI // nc
    cc = cw + 2 * N_STATE
    per = 2 if nc % 2 == 0 else 1
    q = per * length
    chunks = nc // per

    source = hidden.astype(F32).reshape(seqs, length, D)
    normed = rms_scale(source, norm_gain).astype(BF16)
    normed_all = lax.all_gather(normed, "ctx").reshape(nc * mine, D)
    cot = cotangent.reshape(seqs, length, D)
    cot_all = lax.all_gather(cot, "ctx").reshape(nc * mine, D)

    cut = lambda a, start, size, axis: lax.dynamic_slice_in_dim(a, start, size, axis)

    def my_columns(a, axis):
        return jnp.concatenate(
            [cut(a, cw * me_c, cw, axis), lax.slice_in_dim(a, DI, CH, axis=axis)], axis=axis
        )

    in_rows = jnp.concatenate(
        [
            cut(input_weight, cw * me_c, cw, 1),
            cut(input_weight, DI + cw * me_c, cw, 1),
            input_weight[:, 2 * DI : 2 * DI + 2 * N_STATE],
            jnp.pad(
                cut(input_weight, DI + CH + heads * me_c, heads, 1), ((0, 0), (0, LANES - heads))
            ),
        ],
        axis=1,
    )
    in_w = lax.all_gather(in_rows, "fsdp", axis=0, tiled=True)
    shard = output_weight.shape[0]
    offset = cw * me_c - shard * me_f
    held = jnp.logical_and(offset >= 0, offset < shard)
    part = cut(output_weight, jnp.clip(offset, 0, shard - cw), cw, 0)
    out_w = lax.psum(jnp.where(held, part, jnp.zeros_like(part)), "fsdp")

    conv_par = jnp.concatenate(
        [my_columns(conv_w, 1), my_columns(conv_b[None], 1), jnp.zeros((3, cc), F32)], axis=0
    )
    per_head = lambda a: cut(a, heads * me_c, heads, 0)
    pad_heads = lambda a: jnp.pad(a, (0, LANES - heads))[None]
    rate = -jnp.exp(per_head(a_log))
    heads_par = jnp.concatenate(
        [pad_heads(per_head(dt_bias)), pad_heads(rate), jnp.zeros((6, LANES), F32)], axis=0
    )
    chan_par = jnp.concatenate(
        [
            jnp.repeat(per_head(d_skip), HEAD_DIM)[None],
            cut(gate_gain, cw * me_c, cw, 0)[None],
            jnp.zeros((6, cw), F32),
        ],
        axis=0,
    )
    seq_lengths = lengths.reshape(seqs)

    proj = dot(normed_all, in_w).astype(BF16).reshape(nc, seqs, length, -1)
    grad_gated = dot(cot_all, out_w, 1, 1).reshape(nc, seqs, length, cw)
    mixed, pre, states, stats = call_forward(
        cw, per, seq_lengths, proj, conv_par, heads_par, chan_par, grad_gated
    )
    totals = lax.psum(stats[:, :, 0:2], "ctx") / DI
    scale = lax.rsqrt(totals[:, :, 0] + EPS)
    pull = scale * scale * totals[:, :, 1]
    scales = jnp.pad(jnp.stack([scale, pull], axis=2), ((0, 0), (0, 0), (0, 6), (0, 0)))

    by_chunk = lambda a: jnp.moveaxis(
        a.reshape(chunks, seqs, per, length, a.shape[-1]), 2, 1
    ).reshape(nc, seqs, length, a.shape[-1])
    gate = proj[..., :cw].astype(F32)
    g = by_chunk(mixed) * jax.nn.silu(gate)
    gated = (g * by_chunk(scale[..., None]) * chan_par[1]).astype(BF16).reshape(nc * mine, cw)
    branch = dot(gated, out_w).astype(BF16).reshape(nc, mine, D)
    out = lax.psum_scatter(branch, "ctx", scatter_dimension=0).astype(F32) + source.reshape(mine, D)
    grad_out = lax.psum_scatter(
        dot(gated, cot_all, 0, 0).astype(BF16), "fsdp", scatter_dimension=0, tiled=True
    ).astype(F32)

    dproj, dconv, dheads, dchan = call_backward(
        cw, per, seq_lengths, proj, conv_par, heads_par, chan_par, grad_gated, mixed, pre, states,
        scales,
    )
    dproj = dproj.reshape(nc * mine, -1)
    dnormed = dot(dproj, in_w, 1, 1).astype(BF16).reshape(nc, mine, D)
    dnormed = lax.psum_scatter(dnormed, "ctx", scatter_dimension=0).astype(F32)
    _, norm_pull = jax.vjp(rms_scale, source, norm_gain)
    dsource, dnorm_gain = norm_pull(dnormed.reshape(seqs, length, D))
    d_hidden = dsource + cot.astype(F32)

    rows = D // (nc * nf)
    partial = dot(normed_all, dproj, 0, 0).astype(BF16).reshape(nc, nf, rows, -1)
    partial = lax.psum_scatter(partial, "fsdp", scatter_dimension=1)
    pieces = lax.all_to_all(partial, "ctx", split_axis=0, concat_axis=0, tiled=True)
    side = lambda a: jnp.moveaxis(a, 0, 1).reshape(rows, -1)
    grad_in = jnp.concatenate(
        [
            side(pieces[:, :, :cw]),
            side(pieces[:, :, cw : 2 * cw]),
            jnp.sum(pieces[:, :, 2 * cw : 2 * cw + 2 * N_STATE].astype(F32), axis=0).astype(BF16),
            side(pieces[:, :, 2 * cw + 2 * N_STATE : 2 * cw + 2 * N_STATE + heads]),
        ],
        axis=1,
    ).astype(F32)

    place = lambda a, start, size: lax.dynamic_update_slice_in_dim(
        jnp.zeros(a.shape[:-1] + (size,), F32), a, start, a.ndim - 1
    )
    dconv = jnp.concatenate(
        [place(dconv[: CONV_K + 1, :cw], cw * me_c, DI), dconv[: CONV_K + 1, cw:]], axis=1
    )
    dskip = jnp.sum(dchan[0].reshape(heads, HEAD_DIM), axis=1)
    small = (
        dnorm_gain,
        dconv,
        place(dheads[0, :heads], heads * me_c, HEADS),
        place(dheads[1, :heads], heads * me_c, HEADS),
        place(dskip, heads * me_c, HEADS),
        place(dchan[1], cw * me_c, DI),
    )
    dnorm_gain, dconv, dbias, dalog, dskip, dgain = lax.psum(small, ("ctx", "fsdp"))
    shape = hidden.shape
    return (
        out.astype(BF16).reshape(shape),
        d_hidden.reshape(shape),
        dnorm_gain,
        grad_in,
        dconv[:CONV_K],
        dconv[CONV_K],
        dbias,
        dalog,
        dskip,
        dgain,
        grad_out,
    )


def solution(mesh):
    tokens, rows, every = P(None, "fsdp", "ctx", None), P("fsdp", None), P()
    spread = P(("ctx", "fsdp"), None)
    in_specs = (
        tokens, tokens, P(None, "fsdp"), every, rows, every, every, every, every, every, every, rows,
    )
    out_specs = (
        tokens, tokens, every, spread, every, every, every, every, every, every, spread,
    )
    return jax.shard_map(local, mesh=mesh, in_specs=in_specs, out_specs=out_specs, check_vma=False)
```

time: 1680 us -> 615 us (0.37)
  waiting for transfers between devices: 971 us -> 404 us
  matrix products: 239 us -> 46.9 us
  other arithmetic: 190 us -> 23.1 us
  local copies, waits for them, and re-layouts: 129 us -> 21.6 us
  blocking collectives: 109 us -> 56.7 us
  Pallas kernels: 0 us -> 37 us
    all_gather x8 -> x3, waiting for transfers between devices: 809 us -> 85.2 us  [the longest x1 65.7 us: local(): in_w = lax.all_gather(in_rows, 'fsdp', axis=0, tiled=True)]
    dot_general x34 -> x6, matrix products: 239 us -> 46.9 us  [dot(): lax.dot_general(a.astype(BF16), b.astype(BF16), (((ca,), (cb,)), ((), ())...]
    select_n x32 -> x1, other arithmetic: 112 us -> 3.64 us  [local(): out_w = lax.psum(jnp.where(held, part, jnp.zeros_like(part)), 'fsdp')]
    reduce_scatter x2 -> x3, waiting for transfers between devices: 2.22 us -> 91.7 us  [the longest x1 47.9 us: local(): dnormed = lax.psum_scatter(dnormed, 'ctx', scatter_dimension=0).astype(F32)]
    psum x1 -> x2, waiting for transfers between devices: 107 us -> 192 us  [the longest x1 128 us: local(): lax.psum(small, ('ctx', 'fsdp'))]
    mul x49 -> x1, local copies, waits for them, and re-layouts: 61.6 us -> 0.01 us  [local(): g * by_chunk(scale[..., None]) * chan_par[1]]
    all_to_all x1, waiting for transfers between devices: 50.1 us -> 0.01 us  [local(): lax.all_to_all(partial, 'ctx', split_axis=0, concat_axis=0, tiled=True)]
    all_to_all x1 -> x0, blocking collectives: 37.1 us -> none  [local(): lax.all_to_all(normed_all, 'ctx', split_axis=1, concat_axis=0, tiled=True)]
  transfers between devices with their start and end apart: 16 -> 10, of which waited for: 11 -> 8; matrix products, arithmetic and copies ran while one was open for 29% -> 9% of each run, Pallas kernels for 0% -> 0%
where the time goes in v1:
time: 615 us; the launch traced here: 612 us
  waiting for transfers between devices  404 us (66%)
  blocking collectives  56.7 us (9%)
  matrix products  46.9 us (8%)
  Pallas kernels  37 us (6%)
  other arithmetic  23.1 us (4%)
  local copies, waits for them, and re-layouts  21.6 us (4%)
  between operations  16 us (3%)
    psum x1, waiting for transfers between devices, local(): lax.psum(small, ('ctx', 'fsdp'))  128 us
    all_gather x1, waiting for transfers between devices, local(): in_w = lax.all_gather(in_rows, 'fsdp', axis=0, tiled=True)  65.7 us
    psum x1, waiting for transfers between devices, local(): out_w = lax.psum(jnp.where(held, part, jnp.zeros_like(part)), 'fsdp')  63.5 us
    reduce_scatter x1, waiting for transfers between devices, local(): dnormed = lax.psum_scatter(dnormed, 'ctx', scatter_dimension=0).astype(F32)  47.9 us
    dot_general x6, matrix products, dot(): lax.dot_general(a.astype(BF16), b.astype(BF16), (((ca,), (cb,)), ((), ())...  46.9 us
    psum x1, blocking collectives, local(): lax.psum(small, ('ctx', 'fsdp'))  42.6 us
    reduce_scatter x1, waiting for transfers between devices, local(): lax.psum_scatter(dot(gated, cot_all, 0, 0).astype(BF16), 'fsdp', scatter_...  36.6 us
    unnamed x10, waiting for transfers between devices  35.7 us
  transfers between devices with their start and end apart: 10, of which 8 were waited for; matrix products, arithmetic and copies ran while one was open for 9% of the time, Pallas kernels for 0%

profile of v1, /device:TPU:1, one launch (start us, length us, event | category | flops | bytes accessed | tf_op | source)
XLA Modules:
  0.0 611.5 jit_solution(14911277353042481054)
XLA Ops:
  8.1 3.6 dynamic-slice_select_fusion
  20.8 63.5 %all-reduce.9.cloned.1.call-done = bf16[512,2048]{1,0:T(8,128)(2,1)} async-done(((bf16[512,2048]{1,0:T(8,128)(2,1)}), bf16[512,2048]{1,0:T(8,128)(2,1)}) %all-reduce.9.cloned.1.call-update) | async-done | bytes 2097168 | tf_op jit(solution)/shard_map/psum | solution.py:402
  84.4 5.2 convolution_bitcast_fusion
  91.4 19.5 %all-gather.5.cloned.1.call-done = bf16[8,2,64,2048]{3,2,1,0:T(8,128)(2,1)} async-done(((bf16[1,2,64,2048]{3,2,1,0:T(8,128)(2,1)}), bf16[8,2,64,2048]{3,2,1,0:T(8,128)(2,1)}) %all-gather.5.cloned.1.call-update) | async-done | bytes 4194320 | tf_op jit(solution)/shard_map/all_gather | solution.py:375
  110.9 65.7 %all-gather.7.cloned.1.call-done = bf16[2048,1408]{0,1:T(8,128)(2,1)} async-done(((bf16[512,1408]{0,1:T(8,128)(2,1)}), bf16[2048,1408]{0,1:T(8,128)(2,1)}) %all-gather.7.cloned.1.call-update) | async-done | bytes 5767184 | tf_op jit(solution)/shard_map/all_gather | solution.py:397
  176.6 11.3 %convolution_convert_fusion = bf16[1024,1408]{1,0:T(8,128)(2,1)} fusion(bf16[1024,2048]{1,0:T(8,128)(2,1)} %bitcast.132, bf16[2048,1408]{0,1:T(8,128)(2,1)} %all-gather.7.cloned.1.call-done), kind=kOutput, calls=%fused_computation.4 | convolution fusion | flops 5907021824 | bytes 12845056 | tf_op jit(solution)/shard_map/dot_general | solution.py:26
  187.9 13.9 %mixer_forward.1 = (f32[4,2,128,512]{3,2,1,0:T(8,128)}, f32[4,2,128,768]{3,2,1,0:T(8,128)}, f32[4,2,128,512]{3,2,1,0:T(8,128)}, f32[4,2,8,128]{3,2,1,0:T(8,128)}) custom-call(s32[2]{0:T(128)} %bitcast.128, bf16[8,2,64,1408]{3,2,1,0:T(8,128)(2,1)} %bitcast.109, f32[8,768]{1,0:T(8,128)} %maximum_maximum_fusion.conv_w, ...), custom_call_target="tpu_custom_call" | custom-call | tf_op jit(solution)/shard_map/mixer_forward/pallas_call | solution.py:265
  202.5 14.1 %psum.57 = f32[4,2,2,128]{3,2,1,0:T(2,128)S(1)} all-reduce(f32[4,2,2,128]{3,2,1,0:T(2,128)S(1)} %slice.69), channel_id=1, replica_groups=mesh['ctx'=8,'fsdp'=4] {'ctx'}, use_global_device_ids=true, to_apply=%region_2.3 | all-reduce | flops 2048 | bytes 16384 | tf_op jit(solution)/shard_map/psum | solution.py:428
  217.3 23.1 %mixer_backward.1 = (bf16[8,2,64,1408]{3,2,1,0:T(8,128)(2,1)}, f32[8,768]{1,0:T(8,128)}, f32[8,128]{1,0:T(8,128)}, f32[8,512]{1,0:T(8,128)}) custom-call(s32[2]{0:T(128)} %bitcast.129, bf16[8,2,64,1408]{3,2,1,0:T(8,128)(2,1)} %bitcast.110, f32[8,768]{1,0:T(8,128)} %maximum_maximum_fusion.conv_w, f32[8,128]{1,0:T(8,128)} %maximum_maximum_fusion.2.heads_par, ...), custom_call_target="tpu_custom_call" | custom-call | tf_op jit(solution)/shard_map/mixer_backward/pallas_call | solution.py:307
  240.4 9.4 %bitcast_convert_fusion = bf16[2048,1408]{1,0:T(8,128)(2,1)S(1)} fusion(bf16[8,2,64,2048]{3,2,1,0:T(8,128)(2,1)} %all-gather.5.cloned.1.call-done, bf16[8,2,64,1408]{3,2,1,0:T(8,128)(2,1)} %get-tuple-element.23), kind=kOutput, calls=%fused_computation | convolution fusion | flops 5908463616 | bytes 12845056 | tf_op jit(solution)/shard_map/dot_general | solution.py:26
  249.8 3.1 copy.59
  259.2 2.4 fusion.11
  262.6 3.8 bitcast_convert_fusion.1
  266.4 11.1 %convolution_convert_fusion.1 = bf16[1024,2048]{1,0:T(8,128)(2,1)} fusion(bf16[1024,1408]{1,0:T(8,128)(2,1)} %bitcast.133, bf16[2048,1408]{0,1:T(8,128)(2,1)} %all-gather.7.cloned.1.call-done), kind=kOutput, calls=%fused_computation.5 | convolution fusion | flops 5907677184 | bytes 12845056 | tf_op jit(solution)/shard_map/dot_general | solution.py:26
  277.6 6.1 %convolution_convert_fusion.2 = bf16[1024,2048]{1,0:T(8,128)(2,1)} fusion(bf16[1024,512]{1,0:T(8,128)(2,1)S(1)} %bitcast.121, bf16[512,2048]{1,0:T(8,128)(2,1)} %all-reduce.9.cloned.1.call-done), kind=kOutput, calls=%fused_computation.6 | convolution fusion | flops 2149580800 | bytes 7340032 | tf_op jit(solution)/shard_map/dot_general | solution.py:26
  283.8 35.0 %reduce-scatter.13.cloned.1.call-done = bf16[8,1,64,1408]{3,2,0,1:T(8,128)(2,1)} async-done(((bf16[8,4,64,1408]{3,2,0,1:T(8,128)(2,1)}), bf16[8,1,64,1408]{3,2,0,1:T(8,128)(2,1)}) %reduce-scatter.13.cloned.1.call-update) | async-done | bytes 1441808
  318.8 5.3 all-to-all-start
  327.1 128.1 %all-reduce.11.cloned.1.call-done = f32[5,4352]{1,0:T(8,128)} async-done(((f32[5,4352]{1,0:T(8,128)}), f32[5,4352]{1,0:T(8,128)}) %all-reduce.11.cloned.1.call-update) | async-done | bytes 87056 | tf_op jit(solution)/shard_map/psum | solution.py:486
  458.3 36.6 %reduce-scatter.11.cloned.1.call-done = bf16[128,2048]{1,0:T(8,128)(2,1)} async-done(((bf16[512,2048]{1,0:T(8,128)(2,1)}), bf16[128,2048]{1,0:T(8,128)(2,1)}) %reduce-scatter.11.cloned.1.call-update) | async-done | bytes 524304 | tf_op jit(solution)/shard_map/reduce_scatter | solution.py:441
  494.9 2.1 convert_element_type.107
  497.0 47.9 %reduce-scatter.9.cloned.1.call-done = bf16[1,128,2048]{2,1,0:T(8,128)(2,1)} async-done(((bf16[8,128,2048]{2,1,0:T(8,128)(2,1)}), bf16[1,128,2048]{2,1,0:T(8,128)(2,1)}) %reduce-scatter.9.cloned.1.call-update) | async-done | bytes 524304 | tf_op jit(solution)/shard_map/reduce_scatter | solution.py:451
  546.4 42.6 %all-reduce.5 = (f32[2048]{0:T(1024)}, f32[64]{0:T(128)}, f32[64]{0:T(128)}, f32[64]{0:T(128)}, f32[4096]{0:T(1024)}) all-reduce(f32[2048]{0:T(1024)S(1)} %get-tuple-element.71, f32[64]{0:T(128)S(1)} %bitcast_dynamic-update-slice_fusion.1, ...), channel_id=1, replica_groups=mesh['ctx'=8,'fsdp'=4] {'ctx','fsdp'}, use_global_device_ids=true, to_apply=%region_7.8 | all-reduce | flops 6336 | bytes 50688 | tf_op jit(solution)/shard_map/psum | solution.py:486
  589.0 7.3 %reduce-scatter.7.cloned.1.call-done = bf16[1,128,2048]{2,1,0:T(8,128)(2,1)} async-done(((bf16[8,128,2048]{2,1,0:T(8,128)(2,1)}), bf16[1,128,2048]{2,1,0:T(8,128)(2,1)}) %reduce-scatter.7.cloned.1.call-update) | async-done | bytes 524304 | tf_op jit(solution)/shard_map/reduce_scatter | solution.py:440
  596.3 2.6 fusion.17
  (110 shorter events, 32.2 us)
Async XLA Ops:
  8.0 76.3 %all-reduce.9.cloned.1.call-start = ((), (), s32[]{:S(2)}) async-start(), calls=%async_computation.7 | async-start | bytes 4194304 | tf_op jit(solution)/shard_map/psum | solution.py:402
  11.7 1.0 copy-start.1
  11.7 1.2 copy-start.3
  11.7 72.6 %all-gather.9.cloned.1.call-start = ((), (), s32[]{:S(2)}) async-start(), calls=%async_computation.12 | async-start | bytes 4718592 | tf_op jit(solution)/shard_map/all_gather | solution.py:377
  12.3 98.6 %all-gather.5.cloned.1.call-start = ((), (), s32[]{:S(2)}) async-start(), calls=%async_computation.5 | async-start | bytes 4718592 | tf_op jit(solution)/shard_map/all_gather | solution.py:375
  12.9 3.1 slice-start
  14.0 162.6 %all-gather.7.cloned.1.call-start = ((), (), s32[]{:S(2)}) async-start(), calls=%async_computation.6 | async-start | bytes 7208960 | tf_op jit(solution)/shard_map/all_gather | solution.py:397
  16.0 1.4 copy-start.4
  16.0 1.6 copy-start.8
  16.0 1.7 copy-start.9
  16.0 2.7 copy-start.10
  16.0 2.7 copy-start.6
  16.1 4.1 slice-start.1
  17.3 301.5 %reduce-scatter.13.cloned.1.call-start = ((), (), s32[]{:S(2)}) async-start(), calls=%async_computation.13 | async-start | bytes 7208960
  252.9 0.7 copy-start.5
  252.9 2.1 copy-start
  252.9 202.3 %all-reduce.11.cloned.1.call-start = ((), (), s32[]{:S(2)}) async-start(), calls=%async_computation.10 | async-start | bytes 278528 | tf_op jit(solution)/shard_map/psum | solution.py:486
  257.2 237.7 %reduce-scatter.11.cloned.1.call-start = ((), (), s32[]{:S(2)}) async-start(), calls=%async_computation.11 | async-start | bytes 2621440 | tf_op jit(solution)/shard_map/reduce_scatter | solution.py:441
  259.2 3.4 copy-start.7
  266.3 278.6 %reduce-scatter.9.cloned.1.call-start = ((), (), s32[]{:S(2)}) async-start(), calls=%async_computation.9 | async-start | bytes 4718592 | tf_op jit(solution)/shard_map/reduce_scatter | solution.py:451
  277.5 318.8 %reduce-scatter.7.cloned.1.call-start = ((), (), s32[]{:S(2)}) async-start(), calls=%async_computation.8 | async-start | bytes 4718592 | tf_op jit(solution)/shard_map/reduce_scatter | solution.py:440
  318.8 280.1 %all-to-all-start = ((bf16[8,64,1408]{2,1,0:T(8,128)(2,1)}), bf16[8,64,1408]{2,1,0:T(8,128)(2,1)}, u32[]{:S(2)}, u32[]{:S(2)}) async-start(bf16[8,64,1408]{2,1,0:T(8,128)(2,1)} %bitcast.120), calls=%async_computation.2 | async-start | bytes 2883584 | tf_op jit(solution)/shard_map/all_to_all | solution.py:459
  458.3 138.0 %copy-start.2 = (bf16[2,1,64,2048]{3,2,1,0:T(8,128)(2,1)S(1)}, bf16[2,1,64,2048]{3,2,1,0:T(8,128)(2,1)}, u32[]{:S(2)}) copy-start(bf16[2,1,64,2048]{3,2,1,0:T(8,128)(2,1)} %param.13) | copy-start | bytes 1572868
Sparse Core Ops, SparseCore 0:
  12.5 71.7 all-reduce.8
  253.0 65.7 reduce-scatter.12
  325.8 129.3 all-reduce.10
  458.9 35.9 reduce-scatter.10
  497.1 47.8 reduce-scatter.8
  547.1 49.1 reduce-scatter.6
Sparse Core Ops, SparseCore 1:
  13.9 49.2 all-gather.8
  65.3 45.5 all-gather.4
  112.8 63.8 all-gather.6

commit v2 on v1

--- a/solution.py
+++ b/solution.py
@@ -340,6 +340,318 @@
     )(lengths, proj, conv_w, heads_par, chan_par, grad_gated, mixed, pre, states, scales)
 
 
+MESH = pl.DeviceIdType.MESH
+
+
+class push:
+    def __init__(self, src, dst, send_sem, recv_sem, device):
+        self.args = (src, dst, send_sem, recv_sem, device, MESH)
+
+    def start(self):
+        pltpu.make_async_remote_copy(*self.args).start()
+
+    def wait_send(self):
+        pltpu.make_async_remote_copy(*self.args).wait_send()
+
+    def wait_recv(self):
+        pltpu.make_async_remote_copy(*self.args).wait_recv()
+
+    def wait(self):
+        self.wait_send()
+        self.wait_recv()
+
+
+def greet(devices_and_tests):
+    barrier = pltpu.get_barrier_semaphore()
+    count = 0
+    for device, there in devices_and_tests:
+        if there is None:
+            pl.semaphore_signal(barrier, inc=1, device_id=device, device_id_type=MESH)
+            count = count + 1
+        else:
+            @pl.when(there)
+            def _():
+                pl.semaphore_signal(barrier, inc=1, device_id=device, device_id_type=MESH)
+
+            count = count + there.astype(jnp.int32)
+    pl.semaphore_wait(barrier, count)
+
+
+def line_of(nc):
+    me = lax.axis_index("ctx")
+    return nc // 2, me // 2, lax.rem(me, 2)
+
+
+def square_partners():
+    me = lax.axis_index("fsdp")
+    high, low = me // 2, lax.rem(me, 2)
+    return me, high * 2 + (1 - low), (1 - high) * 2 + low
+
+
+def gather_neighbours(nc, nf):
+    nz, z, k = line_of(nc)
+    me_f = lax.axis_index("fsdp")
+    found = [
+        ({"ctx": 2 * z + 1 - k}, None),
+        ({"ctx": 2 * (z + 1) + k}, z < nz - 1),
+        ({"ctx": 2 * (z - 1) + k}, z > 0),
+    ]
+    if nf == 4:
+        _, fx, fy = square_partners()
+        found += [({"fsdp": fx}, None), ({"fsdp": fy}, None)]
+    else:
+        found += [({"fsdp": lax.rem(me_f + j, nf)}, None) for j in range(1, nf)]
+    return found
+
+
+class LineGather:
+    def __init__(self, nc, own, every, sems):
+        self.nz, self.z, self.k = line_of(nc)
+        self.own, self.every = own, every
+        self.up, self.down, self.side, self.got, self.got_side, self.here = sems
+
+    def slot(self, place, core=None):
+        return self.every.at[2 * place + (self.k if core is None else core)]
+
+    def copies(self, d, below):
+        z, k = self.z, self.k
+        origin = z - d if below else z + d
+        src = self.own if d == 0 else self.slot(origin)
+        to = z + 1 if below else z - 1
+        on = push(
+            src, self.slot(origin), (self.up if below else self.down).at[d], self.got.at[origin],
+            {"ctx": 2 * to + k},
+        )
+        side = push(
+            src, self.slot(origin), self.side.at[origin], self.got_side.at[origin],
+            {"ctx": 2 * z + 1 - k},
+        )
+        there = origin >= 0 if below else origin <= self.nz - 1
+        further = to <= self.nz - 1 if below else to >= 0
+        return origin, on, side, there, further
+
+    def begin(self):
+        pltpu.make_async_copy(self.own, self.slot(self.z), self.here).start()
+        for below in (True, False):
+            _, on, side, _, further = self.copies(0, below)
+            pl.when(further)(on.start)
+        side.start()
+
+    def step(self, d):
+        for below in (True, False):
+            origin, on, side, there, further = self.copies(d, below)
+
+            @pl.when(there)
+            def _():
+                on.wait_recv()
+                side.start()
+                pl.when(further)(on.start)
+
+    def end(self):
+        z, k, nz = self.z, self.k, self.nz
+        pltpu.make_async_copy(self.own, self.slot(z), self.here).wait()
+        for place in range(nz):
+            arrived = self.every.at[2 * place + 1 - k]
+            push(
+                arrived, arrived, self.side.at[place], self.got_side.at[place], {"ctx": 2 * z + 1 - k}
+            ).wait()
+        for d in range(nz - 1):
+            for below in (True, False):
+                _, on, _, there, further = self.copies(d, below)
+                pl.when(jnp.logical_and(there, further))(on.wait_send)
+
+
+class SquareGather:
+    def __init__(self, nf, own, every, sems):
+        self.nf, self.own, self.every = nf, own, every
+        self.send, self.got, self.here = sems
+        self.half = own.shape[0] // 2
+
+    def first(self):
+        me = lax.axis_index("fsdp")
+        if self.nf == 4:
+            _, fx, fy = square_partners()
+            peers = [(fx, fx), (fy, fy)]
+        else:
+            peers = [
+                (lax.rem(me + j, self.nf), lax.rem(me + self.nf - j, self.nf))
+                for j in range(1, self.nf)
+            ]
+        return [
+            (
+                push(self.own, self.every.at[me], self.send.at[j], self.got.at[j], {"fsdp": to}),
+                push(self.own, self.every.at[frm], self.send.at[j], self.got.at[j], {"fsdp": to}),
+            )
+            for j, (to, frm) in enumerate(peers)
+        ]
+
+    def second(self):
+        me, fx, fy = square_partners()
+        far = 3 - me
+        pairs = []
+        for j, (via, to) in enumerate(((fx, fy), (fy, fx))):
+            rows = pl.ds(j * self.half, self.half)
+            args = (self.send.at[2 + j], self.got.at[2 + j], {"fsdp": to})
+            there, here = self.every.at[via, rows], self.every.at[far, rows]
+            pairs.append((push(there, there, *args), push(here, here, *args)))
+        return pairs
+
+    def begin(self):
+        me = lax.axis_index("fsdp")
+        pltpu.make_async_copy(self.own, self.every.at[me], self.here).start()
+        for out, _ in self.first():
+            out.start()
+
+    def step(self):
+        for j, (_, arrived) in enumerate(self.first()):
+            arrived.wait_recv()
+            if self.nf == 4:
+                self.second()[j][0].start()
+
+    def end(self):
+        me = lax.axis_index("fsdp")
+        pltpu.make_async_copy(self.own, self.every.at[me], self.here).wait()
+        for out, _ in self.first():
+            out.wait_send()
+        if self.nf == 4:
+            for out, arrived in self.second():
+                arrived.wait_recv()
+                out.wait_send()
+
+
+class Spread:
+    def __init__(self, nf, source, own, every, sems):
+        self.nf, self.source, self.own, self.every = nf, source, own, every
+        self.send, self.got, self.here = sems
+        self.mine = lax.axis_index("fsdp") == source
+
+    def copies(self):
+        me = lax.axis_index("fsdp")
+        return [
+            push(
+                self.own, self.every, self.send.at[j], self.got.at[0], {"fsdp": lax.rem(me + j, self.nf)}
+            )
+            for j in range(1, self.nf)
+        ]
+
+    def begin(self):
+        @pl.when(self.mine)
+        def _():
+            pltpu.make_async_copy(self.own, self.every, self.here).start()
+            for out in self.copies():
+                out.start()
+
+    def step(self):
+        pass
+
+    def end(self):
+        @pl.when(self.mine)
+        def _():
+            pltpu.make_async_copy(self.own, self.every, self.here).wait()
+            for out in self.copies():
+                out.wait_send()
+
+        if self.nf > 1:
+
+            @pl.when(jnp.logical_not(self.mine))
+            def _():
+                self.copies()[0].wait_recv()
+
+
+def gather_kernel(
+    nc, nf, spread, normed, cot, in_rows, out_rows, normed_all, cot_all, in_all, out_all,
+    line_sems, in_sems, out_sems, here,
+):
+    nz = nc // 2
+    lines = [
+        LineGather(
+            nc, own, every, [line_sems.at[i, j] for j in range(5)] + [here.at[i]]
+        )
+        for i, (own, every) in enumerate(((normed, normed_all), (cot, cot_all)))
+    ]
+    weights = SquareGather(nf, in_rows, in_all, [in_sems.at[0], in_sems.at[1], here.at[2]])
+    out_args = (out_rows, out_all, [out_sems.at[0], out_sems.at[1], here.at[3]])
+    if spread:
+        outs = Spread(nf, lax.axis_index("ctx") // spread, *out_args)
+    else:
+        outs = SquareGather(nf, *out_args)
+    greet(gather_neighbours(nc, nf))
+    weights.begin()
+    lines[0].begin()
+    for d in range(1, nz):
+        lines[0].step(d)
+        if d == 1:
+            lines[1].begin()
+    weights.step()
+    outs.begin()
+    for d in range(1, nz):
+        lines[1].step(d)
+    if nz == 1:
+        lines[1].begin()
+    outs.step()
+    for part in (weights, lines[0], lines[1], outs):
+        part.end()
+
+
+def call_gather(nc, nf, spread, normed, cot, in_rows, out_rows):
+    every = lambda a, n: jax.ShapeDtypeStruct((n,) + a.shape, a.dtype)
+    nz = nc // 2
+    places = max(nf, 4)
+    anywhere = pl.BlockSpec(memory_space=pl.ANY)
+    return pl.pallas_call(
+        functools.partial(gather_kernel, nc, nf, spread),
+        in_specs=[anywhere] * 4,
+        out_specs=[anywhere] * 4,
+        out_shape=[
+            every(normed, nc),
+            every(cot, nc),
+            every(in_rows, nf),
+            jax.ShapeDtypeStruct(out_rows.shape, BF16) if spread else every(out_rows, nf),
+        ],
+        scratch_shapes=[
+            pltpu.SemaphoreType.DMA((2, 5, nz)),
+            pltpu.SemaphoreType.DMA((2, places)),
+            pltpu.SemaphoreType.DMA((2, places)),
+            pltpu.SemaphoreType.DMA((4,)),
+        ],
+        compiler_params=pltpu.CompilerParams(
+            collective_id=0, has_side_effects=True, vmem_limit_bytes=VMEM_LIMIT
+        ),
+        name="gather",
+    )(normed, cot, in_rows, out_rows)
+
+
+def add_over_ctx_kernel(nc, own, total, held, send, got):
+    me = lax.axis_index("ctx")
+    peers = [(lax.rem(me + j, nc), lax.rem(me + nc - j, nc)) for j in range(1, nc)]
+    greet([({"ctx": to}, None) for to, _ in peers])
+    for j, (to, _) in enumerate(peers):
+        push(own, held.at[me], send.at[j], got.at[j], {"ctx": to}).start()
+    held[me] = own[...]
+    for j, (to, frm) in enumerate(peers):
+        push(own, held.at[frm], send.at[j], got.at[j], {"ctx": to}).wait()
+    result = held[0]
+    for c in range(1, nc):
+        result = result + held[c]
+    total[...] = result
+
+
+def add_over_ctx(nc, own):
+    return pl.pallas_call(
+        functools.partial(add_over_ctx_kernel, nc),
+        in_specs=[pl.BlockSpec(memory_space=pltpu.VMEM)],
+        out_specs=pl.BlockSpec(memory_space=pltpu.VMEM),
+        out_shape=jax.ShapeDtypeStruct(own.shape, F32),
+        scratch_shapes=[
+            pltpu.VMEM((nc,) + own.shape, F32),
+            pltpu.SemaphoreType.DMA((nc,)),
+            pltpu.SemaphoreType.DMA((nc,)),
+        ],
+        compiler_params=pltpu.CompilerParams(collective_id=1, has_side_effects=True),
+        name="add_over_ctx",
+    )(own)
+
+
 def rms_scale(values, gain_vec):
     return values * lax.rsqrt(jnp.mean(values * values, axis=-1, keepdims=True) + EPS) * gain_vec
 
@@ -370,41 +682,53 @@
     q = per * length
     chunks = nc // per
 
+    span = nf if (DI // nf // nc) % LANES == 0 else 1
+    wide, apart = cw // span, DI // span
+    cut = lambda a, start, size, axis: lax.dynamic_slice_in_dim(a, start, size, axis)
+
+    def my_blocks(a, base, axis, unit):
+        return jnp.concatenate(
+            [
+                cut(a, base + (i * apart + wide * me_c) // unit, wide // unit, axis)
+                for i in range(span)
+            ],
+            axis=axis,
+        )
+
     source = hidden.astype(F32).reshape(seqs, length, D)
     normed = rms_scale(source, norm_gain).astype(BF16)
-    normed_all = lax.all_gather(normed, "ctx").reshape(nc * mine, D)
-    cot = cotangent.reshape(seqs, length, D)
-    cot_all = lax.all_gather(cot, "ctx").reshape(nc * mine, D)
-
-    cut = lambda a, start, size, axis: lax.dynamic_slice_in_dim(a, start, size, axis)
-
-    def my_columns(a, axis):
-        return jnp.concatenate(
-            [cut(a, cw * me_c, cw, axis), lax.slice_in_dim(a, DI, CH, axis=axis)], axis=axis
-        )
-
+    cot = cotangent.reshape(mine, D)
     in_rows = jnp.concatenate(
         [
-            cut(input_weight, cw * me_c, cw, 1),
-            cut(input_weight, DI + cw * me_c, cw, 1),
+            my_blocks(input_weight, 0, 1, 1),
+            my_blocks(input_weight, DI, 1, 1),
             input_weight[:, 2 * DI : 2 * DI + 2 * N_STATE],
             jnp.pad(
-                cut(input_weight, DI + CH + heads * me_c, heads, 1), ((0, 0), (0, LANES - heads))
+                my_blocks(input_weight, DI + CH, 1, HEAD_DIM), ((0, 0), (0, LANES - heads))
             ),
         ],
         axis=1,
     )
-    in_w = lax.all_gather(in_rows, "fsdp", axis=0, tiled=True)
     shard = output_weight.shape[0]
-    offset = cw * me_c - shard * me_f
-    held = jnp.logical_and(offset >= 0, offset < shard)
-    part = cut(output_weight, jnp.clip(offset, 0, shard - cw), cw, 0)
-    out_w = lax.psum(jnp.where(held, part, jnp.zeros_like(part)), "fsdp")
-
+    if span > 1:
+        out_rows = cut(output_weight, wide * me_c, wide, 0)
+        spread = 0
+    else:
+        spread = shard // cw
+        out_rows = cut(output_weight, cw * lax.rem(me_c, spread), cw, 0)
+    normed_all, cot_all, in_w, out_w = call_gather(
+        nc, nf, spread, normed.reshape(mine, D), cot, in_rows, out_rows
+    )
+    normed_all, cot_all = normed_all.reshape(nc * mine, D), cot_all.reshape(nc * mine, D)
+    in_w, out_w = in_w.reshape(D, -1), out_w.reshape(cw, D)
+
+    my_columns = lambda a: jnp.concatenate(
+        [my_blocks(a, 0, 1, 1), lax.slice_in_dim(a, DI, CH, axis=1)], axis=1
+    )
     conv_par = jnp.concatenate(
-        [my_columns(conv_w, 1), my_columns(conv_b[None], 1), jnp.zeros((3, cc), F32)], axis=0
-    )
-    per_head = lambda a: cut(a, heads * me_c, heads, 0)
+        [my_columns(conv_w), my_columns(conv_b[None]), jnp.zeros((3, cc), F32)], axis=0
+    )
+    per_head = lambda a: my_blocks(a, 0, 0, HEAD_DIM)
     pad_heads = lambda a: jnp.pad(a, (0, LANES - heads))[None]
     rate = -jnp.exp(per_head(a_log))
     heads_par = jnp.concatenate(
@@ -413,7 +737,7 @@
     chan_par = jnp.concatenate(
         [
             jnp.repeat(per_head(d_skip), HEAD_DIM)[None],
-            cut(gate_gain, cw * me_c, cw, 0)[None],
+            my_blocks(gate_gain, 0, 0, 1)[None],
             jnp.zeros((6, cw), F32),
         ],
         axis=0,
@@ -425,7 +749,8 @@
     mixed, pre, states, stats = call_forward(
         cw, per, seq_lengths, proj, conv_par, heads_par, chan_par, grad_gated
     )
-    totals = lax.psum(stats[:, :, 0:2], "ctx") / DI
+    totals = add_over_ctx(nc, stats[:, :, 0:2].reshape(chunks * seqs * 2, q)) / DI
+    totals = totals.reshape(chunks, seqs, 2, q)
     scale = lax.rsqrt(totals[:, :, 0] + EPS)
     pull = scale * scale * totals[:, :, 1]
     scales = jnp.pad(jnp.stack([scale, pull], axis=2), ((0, 0), (0, 0), (0, 6), (0, 0)))
@@ -440,7 +765,11 @@
     out = lax.psum_scatter(branch, "ctx", scatter_dimension=0).astype(F32) + source.reshape(mine, D)
     grad_out = lax.psum_scatter(
         dot(gated, cot_all, 0, 0).astype(BF16), "fsdp", scatter_dimension=0, tiled=True
-    ).astype(F32)
+    )
+    if span > 1:
+        route = [(c * nf + f, f * nc + c) for c in range(nc) for f in range(nf)]
+        grad_out = lax.ppermute(grad_out, ("ctx", "fsdp"), route)
+    grad_out = grad_out.astype(F32)
 
     dproj, dconv, dheads, dchan = call_backward(
         cw, per, seq_lengths, proj, conv_par, heads_par, chan_par, grad_gated, mixed, pre, states,
@@ -451,13 +780,15 @@
     dnormed = lax.psum_scatter(dnormed, "ctx", scatter_dimension=0).astype(F32)
     _, norm_pull = jax.vjp(rms_scale, source, norm_gain)
     dsource, dnorm_gain = norm_pull(dnormed.reshape(seqs, length, D))
-    d_hidden = dsource + cot.astype(F32)
+    d_hidden = dsource + cot.astype(F32).reshape(seqs, length, D)
 
     rows = D // (nc * nf)
     partial = dot(normed_all, dproj, 0, 0).astype(BF16).reshape(nc, nf, rows, -1)
     partial = lax.psum_scatter(partial, "fsdp", scatter_dimension=1)
     pieces = lax.all_to_all(partial, "ctx", split_axis=0, concat_axis=0, tiled=True)
-    side = lambda a: jnp.moveaxis(a, 0, 1).reshape(rows, -1)
+    side = lambda a: jnp.transpose(
+        a.reshape(nc, rows, span, -1), (1, 2, 0, 3)
+    ).reshape(rows, -1)
     grad_in = jnp.concatenate(
         [
             side(pieces[:, :, :cw]),
@@ -468,20 +799,27 @@
         axis=1,
     ).astype(F32)
 
-    place = lambda a, start, size: lax.dynamic_update_slice_in_dim(
-        jnp.zeros(a.shape[:-1] + (size,), F32), a, start, a.ndim - 1
-    )
+    def place(a, unit):
+        axis, size = a.ndim - 1, wide // unit
+        whole = jnp.zeros(a.shape[:-1] + (DI // unit,), F32)
+        for i in range(span):
+            part = lax.slice_in_dim(a, i * size, (i + 1) * size, axis=axis)
+            whole = lax.dynamic_update_slice_in_dim(
+                whole, part, (i * apart + wide * me_c) // unit, axis
+            )
+        return whole
+
     dconv = jnp.concatenate(
-        [place(dconv[: CONV_K + 1, :cw], cw * me_c, DI), dconv[: CONV_K + 1, cw:]], axis=1
+        [place(dconv[: CONV_K + 1, :cw], 1), dconv[: CONV_K + 1, cw:]], axis=1
     )
     dskip = jnp.sum(dchan[0].reshape(heads, HEAD_DIM), axis=1)
     small = (
         dnorm_gain,
         dconv,
-        place(dheads[0, :heads], heads * me_c, HEADS),
-        place(dheads[1, :heads], heads * me_c, HEADS),
-        place(dskip, heads * me_c, HEADS),
-        place(dchan[1], cw * me_c, DI),
+        place(dheads[0, :heads], HEAD_DIM),
+        place(dheads[1, :heads], HEAD_DIM),
+        place(dskip, HEAD_DIM),
+        place(dchan[1], 1),
     )
     dnorm_gain, dconv, dbias, dalog, dskip, dgain = lax.psum(small, ("ctx", "fsdp"))
     shape = hidden.shape

time: 615 us -> 464 us (0.75)
  waiting for transfers between devices: 404 us -> 153 us
  Pallas kernels: 37 us -> 140 us
  local copies, waits for them, and re-layouts: 21.6 us -> 30.3 us
  blocking collectives: 56.7 us -> 50.2 us
    pallas_call x0 -> x2, Pallas kernels: none -> 103 us  [the longest x1 95.1 us: call_gather(): pl.pallas_call(functools.partial(gather_kernel, nc, nf, spread), in_specs...]
    all_gather x3 -> x0, waiting for transfers between devices: 85.2 us -> none  [the longest x1 65.7 us: local(): in_w = lax.all_gather(in_rows, 'fsdp', axis=0, tiled=True)]
    psum x1 -> x0, waiting for transfers between devices: 63.5 us -> none  [local(): out_w = lax.psum(jnp.where(held, part, jnp.zeros_like(part)), 'fsdp')]
    reduce_scatter x1, waiting for transfers between devices: 47.9 us -> 0.01 us  [local(): dnormed = lax.psum_scatter(dnormed, 'ctx', scatter_dimension=0).astype(F32)]
    psum x1, waiting for transfers between devices: 128 us -> 84.7 us  [local(): lax.psum(small, ('ctx', 'fsdp'))]
    psum x1 -> x0, blocking collectives: 14.1 us -> none  [local(): totals = lax.psum(stats[:, :, 0:2], 'ctx') / DI]
    psum x1, blocking collectives: 42.6 us -> 50.2 us  [local(): lax.psum(small, ('ctx', 'fsdp'))]
    reduce_scatter x1, waiting for transfers between devices: 7.26 us -> 0.01 us  [local(): lax.psum_scatter(branch, 'ctx', scatter_dimension=0).astype(F32)]
  transfers between devices with their start and end apart: 10 -> 7, of which waited for: 8 -> 3; matrix products, arithmetic and copies ran while one was open for 9% -> 8% of each run, Pallas kernels for 0% -> 0%
where the time goes in v2:
time: 464 us; the launch traced here: 462 us
  waiting for transfers between devices  153 us (33%)
  Pallas kernels  140 us (30%)
  blocking collectives  50.2 us (11%)
  matrix products  45.4 us (10%)
  local copies, waits for them, and re-layouts  30.3 us (7%)
  other arithmetic  17.3 us (4%)
  between operations  15.8 us (3%)
  starting transfers between devices  9.37 us (2%)
    pallas_call x1, Pallas kernels, call_gather(): pl.pallas_call(functools.partial(gather_kernel, nc, nf, spread), in_specs...  95.1 us
    psum x1, waiting for transfers between devices, local(): lax.psum(small, ('ctx', 'fsdp'))  84.7 us
    psum x1, blocking collectives, local(): lax.psum(small, ('ctx', 'fsdp'))  50.2 us
    dot_general x6, matrix products, dot(): lax.dot_general(a.astype(BF16), b.astype(BF16), (((ca,), (cb,)), ((), ())...  45.4 us
    unnamed x6, waiting for transfers between devices  37 us
    reduce_scatter x1, waiting for transfers between devices, local(): lax.psum_scatter(dot(gated, cot_all, 0, 0).astype(BF16), 'fsdp', scatter_...  31 us
    pallas_call x1, Pallas kernels, call_backward(): pl.pallas_call(functools.partial(backward_kernel, cw, chunks), grid=(chun...  23.4 us
    pallas_call x1, Pallas kernels, call_forward(): pl.pallas_call(functools.partial(forward_kernel, cw), grid=(chunks,), in_...  13.9 us
  transfers between devices with their start and end apart: 7, of which 3 were waited for; matrix products, arithmetic and copies ran while one was open for 8% of the time, Pallas kernels for 0%

profile of v2, /device:TPU:1, one launch (start us, length us, event | category | flops | bytes accessed | tf_op | source)
XLA Modules:
  0.0 461.5 jit_solution(12231585636765557154)
XLA Ops:
  9.4 1.4 constant_dynamic-slice_fusion.9
  19.0 2.3 constant_dynamic-slice_fusion.4.out_rows
  21.2 95.1 %gather.1 = (bf16[8,128,2048]{2,1,0:T(8,128)(2,1)}, bf16[8,128,2048]{2,1,0:T(8,128)(2,1)}, bf16[4,512,1408]{2,1,0:T(8,128)(2,1)}, bf16[4,128,2048]{2,1,0:T(8,128)(2,1)}) custom-call(bf16[128,2048]{1,0:T(8,128)(2,1)} %fusion.14.normed, bf16[128,2048]{1,0:T(8,128)(2,1)} %bitcast.127, bf16[512,1408]{1,0:T(8,128)(2,1)} %copy-done.3, ...), custom_call_target="tpu_custom_call" | custom-call | tf_op jit(solution)/shard_map/gather/pallas_call | solution.py:601
  116.4 11.4 %convolution_convert_fusion.1 = bf16[1024,1408]{1,0:T(8,128)(2,1)} fusion(bf16[1024,2048]{1,0:T(8,128)(2,1)} %bitcast.144, bf16[2048,1408]{1,0:T(8,128)(2,1)} %bitcast.140), kind=kOutput, calls=%fused_computation.1 | convolution fusion | flops 5907021824 | bytes 12845056 | tf_op jit(solution)/shard_map/dot_general | solution.py:26
  130.0 3.7 fusion.26.grad_gated
  134.4 13.9 %mixer_forward.1 = (f32[4,2,128,512]{3,2,1,0:T(8,128)}, f32[4,2,128,768]{3,2,1,0:T(8,128)}, f32[4,2,128,512]{3,2,1,0:T(8,128)}, f32[4,2,8,128]{3,2,1,0:T(8,128)}) custom-call(s32[2]{0:T(128)} %bitcast.138, bf16[8,2,64,1408]{3,2,1,0:T(8,128)(2,1)} %bitcast.112, f32[8,768]{1,0:T(8,128)} %maximum_maximum_fusion.conv_w, ...), custom_call_target="tpu_custom_call" | custom-call | tf_op jit(solution)/shard_map/mixer_forward/pallas_call | solution.py:265
  149.6 8.1 %add_over_ctx.1 = f32[16,128]{1,0:T(8,128)} custom-call(f32[16,128]{1,0:T(8,128)} %bitcast.135), custom_call_target="tpu_custom_call" | custom-call | tf_op jit(solution)/shard_map/add_over_ctx/pallas_call | solution.py:640
  159.1 23.4 %mixer_backward.1 = (bf16[8,2,64,1408]{3,2,1,0:T(8,128)(2,1)}, f32[8,768]{1,0:T(8,128)}, f32[8,128]{1,0:T(8,128)}, f32[8,512]{1,0:T(8,128)}) custom-call(s32[2]{0:T(128)} %bitcast.139, bf16[8,2,64,1408]{3,2,1,0:T(8,128)(2,1)} %bitcast.113, f32[8,768]{1,0:T(8,128)} %maximum_maximum_fusion.conv_w, f32[8,128]{1,0:T(8,128)} %maximum_maximum_fusion.2.heads_par, ...), custom_call_target="tpu_custom_call" | custom-call | tf_op jit(solution)/shard_map/mixer_backward/pallas_call | solution.py:307
  182.5 9.4 %convolution_convert_fusion = bf16[2048,1408]{1,0:T(8,128)(2,1)S(1)} fusion(bf16[1024,2048]{1,0:T(8,128)(2,1)} %bitcast.145, bf16[1024,1408]{1,0:T(8,128)(2,1)} %bitcast.146), kind=kOutput, calls=%fused_computation | convolution fusion | flops 5908463616 | bytes 12845056 | tf_op jit(solution)/shard_map/dot_general | solution.py:26
  191.9 3.1 copy.71
  196.9 2.1 fusion.6
  199.4 3.8 convolution_convert_fusion.4
  204.8 10.9 %convolution_convert_fusion.2 = bf16[1024,2048]{1,0:T(8,128)(2,1)} fusion(bf16[1024,1408]{1,0:T(8,128)(2,1)} %bitcast.147, bf16[2048,1408]{1,0:T(8,128)(2,1)} %bitcast.141), kind=kOutput, calls=%fused_computation.2 | convolution fusion | flops 5907677184 | bytes 12845056 | tf_op jit(solution)/shard_map/dot_general | solution.py:26
  215.8 6.2 %convolution_convert_fusion.3 = bf16[1024,2048]{1,0:T(8,128)(2,1)} fusion(bf16[1024,512]{1,0:T(8,128)(2,1)S(1)} %bitcast.130, bf16[512,2048]{1,0:T(8,128)(2,1)} %bitcast.148), kind=kOutput, calls=%fused_computation.3 | convolution fusion | flops 2149580800 | bytes 7340032 | tf_op jit(solution)/shard_map/dot_general | solution.py:26
  223.8 37.0 %reduce-scatter.13.cloned.1.call-done = bf16[8,1,64,1408]{3,2,0,1:T(8,128)(2,1)} async-done(((bf16[8,4,64,1408]{3,2,0,1:T(8,128)(2,1)}), bf16[8,1,64,1408]{3,2,0,1:T(8,128)(2,1)}) %reduce-scatter.13.cloned.1.call-update) | async-done | bytes 1441808
  260.7 5.4 %all-to-all-start = ((bf16[8,64,1408]{2,1,0:T(8,128)(2,1)}), bf16[8,64,1408]{2,1,0:T(8,128)(2,1)}, u32[]{:S(2)}, u32[]{:S(2)}) async-start(bf16[8,64,1408]{2,1,0:T(8,128)(2,1)} %bitcast.128), calls=%async_computation.2 | async-start | bytes 2883584 | tf_op jit(solution)/shard_map/all_to_all | solution.py:788
  268.7 31.0 %reduce-scatter.11.cloned.1.call-done = bf16[128,2048]{1,0:T(8,128)(2,1)} async-done(((bf16[512,2048]{1,0:T(8,128)(2,1)}), bf16[128,2048]{1,0:T(8,128)(2,1)}) %reduce-scatter.11.cloned.1.call-update) | async-done | bytes 524304 | tf_op jit(solution)/shard_map/reduce_scatter | solution.py:766
  299.7 3.6 collective-permute-start
  304.3 84.7 %all-reduce.8.cloned.1.call-done = f32[5,4352]{1,0:T(8,128)} async-done(((f32[5,4352]{1,0:T(8,128)}), f32[5,4352]{1,0:T(8,128)}) %all-reduce.8.cloned.1.call-update) | async-done | bytes 87056 | tf_op jit(solution)/shard_map/psum | solution.py:824
  388.9 1.6 slice.224
  390.5 1.6 slice_reduce_fusion.1
  394.7 50.2 %all-reduce.5 = (f32[2048]{0:T(1024)}, f32[64]{0:T(128)}, f32[64]{0:T(128)}, f32[64]{0:T(128)}, f32[4096]{0:T(1024)}) all-reduce(f32[2048]{0:T(1024)S(1)} %get-tuple-element.35, f32[64]{0:T(128)S(1)} %bitcast_dynamic-update-slice_fusion.8, f32[64]{0:T(128)S(1)} %get-tuple-element.66, ...), channel_id=1, replica_groups=mesh['ctx'=8,'fsdp'=4] {'ctx','fsdp'}, use_global_device_ids=true, to_apply=%region_5.6 | all-reduce | flops 6336 | bytes 50688 | tf_op jit(solution)/shard_map/psum | solution.py:824
  444.9 2.6 fusion.7
  452.9 1.5 maximum_convert_fusion
  (152 shorter events, 32.1 us)
Async XLA Ops:
  8.0 252.7 %reduce-scatter.13.cloned.1.call-start = ((), (), s32[]{:S(2)}) async-start(), calls=%async_computation.9 | async-start | bytes 7208960
  9.4 2.5 slice-start
  9.4 3.7 copy-start.6
  10.9 6.1 %copy-start.7 = (f32[64]{0:T(128)S(1)}, f32[64]{0:T(128)}, u32[]{:S(2)}) copy-start(f32[64]{0:T(128)} %param.20) | copy-start | bytes 772
  10.9 6.4 %copy-start.8 = (f32[64]{0:T(128)S(1)}, f32[64]{0:T(128)}, u32[]{:S(2)}) copy-start(f32[64]{0:T(128)} %param.21) | copy-start | bytes 772
  10.9 6.4 %copy-start.9 = (f32[64]{0:T(128)S(1)}, f32[64]{0:T(128)}, u32[]{:S(2)}) copy-start(f32[64]{0:T(128)} %param.19) | copy-start | bytes 772
  10.9 6.7 %copy-start.1 = (bf16[2,1,64,2048]{3,2,1,0:T(8,128)(2,1)S(1)}, bf16[2,1,64,2048]{3,2,1,0:T(8,128)(2,1)}, u32[]{:S(2)}) copy-start(bf16[2,1,64,2048]{3,2,1,0:T(8,128)(2,1)} %param.12) | copy-start | bytes 1572868
  10.9 6.7 %copy-start.4 = (f32[2048]{0:T(1024)S(1)}, f32[2048]{0:T(1024)}, u32[]{:S(2)}) copy-start(f32[2048]{0:T(1024)} %param.15) | copy-start | bytes 24580
  18.9 2.3 copy-start.3
  116.3 13.6 %copy-start.11 = (bf16[8,128,2048]{2,1,0:T(8,128)(2,1)S(1)}, bf16[8,128,2048]{2,1,0:T(8,128)(2,1)}, u32[]{:S(2)}) copy-start(bf16[8,128,2048]{2,1,0:T(8,128)(2,1)} %get-tuple-element.25) | copy-start | bytes 12582916
  116.4 13.6 %copy-start.13 = (bf16[4,128,2048]{2,1,0:T(8,128)(2,1)S(1)}, bf16[4,128,2048]{2,1,0:T(8,128)(2,1)}, u32[]{:S(2)}) copy-start(bf16[4,128,2048]{2,1,0:T(8,128)(2,1)} %get-tuple-element.26) | copy-start | bytes 6291460
  194.9 1.6 copy-start
  195.0 104.8 %reduce-scatter.11.cloned.1.call-start = ((), (), s32[]{:S(2)}) async-start(), calls=%async_computation.8 | async-start | bytes 2621440 | tf_op jit(solution)/shard_map/reduce_scatter | solution.py:766
  196.9 2.5 copy-start.12
  203.2 0.7 copy-start.5
  203.2 185.7 %all-reduce.8.cloned.1.call-start = ((), (), s32[]{:S(2)}) async-start(), calls=%async_computation.7 | async-start | bytes 278528 | tf_op jit(solution)/shard_map/psum | solution.py:824
  204.7 188.4 %reduce-scatter.9.cloned.1.call-start = ((), (), s32[]{:S(2)}) async-start(), calls=%async_computation.6 | async-start | bytes 4718592 | tf_op jit(solution)/shard_map/reduce_scatter | solution.py:780
  215.7 229.2 %reduce-scatter.7.cloned.1.call-start = ((), (), s32[]{:S(2)}) async-start(), calls=%async_computation.5 | async-start | bytes 4718592 | tf_op jit(solution)/shard_map/reduce_scatter | solution.py:765
  222.0 1.2 copy-start.10
  260.7 186.8 %all-to-all-start = ((bf16[8,64,1408]{2,1,0:T(8,128)(2,1)}), bf16[8,64,1408]{2,1,0:T(8,128)(2,1)}, u32[]{:S(2)}, u32[]{:S(2)}) async-start(bf16[8,64,1408]{2,1,0:T(8,128)(2,1)} %bitcast.128), calls=%async_computation.2 | async-start | bytes 2883584 | tf_op jit(solution)/shard_map/all_to_all | solution.py:788
  299.7 92.3 %collective-permute-start = (bf16[128,2048]{1,0:T(8,128)(2,1)}, bf16[128,2048]{1,0:T(8,128)(2,1)S(1)}, u32[]{:S(2)}, u32[]{:S(2)}) collective-permute-start(bf16[128,2048]{1,0:T(8,128)(2,1)} %reduce-scatter.11.cloned.1.call-done), channel_id=1, source_target_pairs={{0,0},{1,8},{2,16},{3,24},{4,1},{5,9},{6,17},{7,25},{8,2},{9,10},{... | collective-permute-start | bytes 1572872 | tf_op jit(solution)/shard_map/ppermute | solution.py:771
  392.1 52.9 %copy-start.2 = (bf16[2,1,64,2048]{3,2,1,0:T(8,128)(2,1)S(1)}, bf16[2,1,64,2048]{3,2,1,0:T(8,128)(2,1)}, u32[]{:S(2)}) copy-start(bf16[2,1,64,2048]{3,2,1,0:T(8,128)(2,1)} %param.13) | copy-start | bytes 1572868
Sparse Core Ops, SparseCore 0:
  195.1 65.6 reduce-scatter.12
  264.3 35.4 reduce-scatter.10
  302.1 78.7 reduce-scatter.8
  383.2 48.0 reduce-scatter.6
Sparse Core Ops, SparseCore 1:
  210.8 178.1 all-reduce.7

commit v3 on v2

--- a/solution.py
+++ b/solution.py
@@ -652,6 +652,365 @@
     )(own)
 
 
+def add_rows(into, other, rows=16):
+    def body(i, _):
+        at = pl.ds(pl.multiple_of(i * rows, rows), rows)
+        into[at] = (into[at].astype(F32) + other[at].astype(F32)).astype(into.dtype)
+        return 0
+
+    lax.fori_loop(0, into.shape[0] // rows, body, 0)
+
+
+class LineReduce:
+    def __init__(self, nc, parts, acc, landed, sems):
+        self.nz, self.z, self.k = line_of(nc)
+        self.parts, self.acc, self.landed = parts, acc, landed
+        self.side, self.got_side, self.send, self.got = sems
+
+    def to_side(self, place):
+        other = {"ctx": 2 * self.z + 1 - self.k}
+        return push(
+            self.parts.at[2 * place + 1 - self.k], self.acc.at[place], self.side.at[place],
+            self.got_side.at[place], other,
+        )
+
+    def begin(self):
+        for place in range(self.nz):
+            self.to_side(place).start()
+
+    def merge(self):
+        for place in range(self.nz):
+            self.to_side(place).wait_recv()
+            add_rows(self.acc.at[place], self.parts.at[2 * place + self.k])
+
+    def along(self, place, up):
+        way = 0 if up else 1
+        return push(
+            self.acc.at[place], self.landed.at[way, place], self.send.at[way, place],
+            self.got.at[way, place], {"ctx": 2 * (self.z + (1 if up else -1)) + self.k},
+        )
+
+    def arrive(self, place, up, into):
+        self.along(place, up).wait_recv()
+        add_rows(into, self.landed.at[0 if up else 1, place])
+
+    def moves(self):
+        for i in range(self.nz - 1):
+            yield i, self.nz - 1 - i, True
+            yield i, i, False
+
+    def step(self, i):
+        z, nz = self.z, self.nz
+        for at, place, up in self.moves():
+            if at != i:
+                continue
+
+            @pl.when(z < place if up else z > place)
+            def _():
+                @pl.when(z > 0 if up else z < nz - 1)
+                def _():
+                    self.arrive(place, up, self.acc.at[place])
+
+                self.along(place, up).start()
+
+    def final(self, total):
+        z, nz = self.z, self.nz
+        total[...] = self.acc[z].astype(F32)
+
+        @pl.when(z > 0)
+        def _():
+            self.arrive(z, True, total)
+
+        @pl.when(z < nz - 1)
+        def _():
+            self.arrive(z, False, total)
+
+    def end(self):
+        for place in range(self.nz):
+            self.to_side(place).wait_send()
+        for _, place, up in self.moves():
+            pl.when(self.z < place if up else self.z > place)(self.along(place, up).wait_send)
+
+
+class SquareReduce:
+    def __init__(self, nf, parts, landed, total, sems):
+        self.nf, self.parts, self.landed, self.total = nf, parts, landed, total
+        self.send, self.got = sems
+        self.half = parts.shape[1] // 2
+
+    @staticmethod
+    def landing(nf, shape):
+        blocks, rows, cols = shape
+        return (6, blocks // 2, rows, cols) if nf == 4 else (nf, blocks, rows, cols)
+
+    def copy(self, n, src, to):
+        return push(src, self.landed.at[n], self.send.at[n], self.got.at[n], {"fsdp": to})
+
+    def way(self, h):
+        me, fx, fy = square_partners()
+        first, second = (fx, fy) if h == 0 else (fy, fx)
+        return me, first, second, pl.ds(h * self.half, self.half)
+
+    def firsts(self, h):
+        me, first, second, at = self.way(h)
+        return (
+            self.copy(3 * h, self.parts.at[3 - me, at], first),
+            self.copy(3 * h + 1, self.parts.at[first, at], first),
+        )
+
+    def second_(self, h):
+        _, _, second, _ = self.way(h)
+        return self.copy(3 * h + 2, self.landed.at[3 * h], second)
+
+    def others(self):
+        me = lax.axis_index("fsdp")
+        tos = [lax.rem(me + j, self.nf) for j in range(1, self.nf)]
+        return [self.copy(j + 1, self.parts.at[to], to) for j, to in enumerate(tos)]
+
+    def begin(self):
+        if self.nf == 4:
+            for i in range(2):
+                for h in range(2):
+                    self.firsts(h)[i].start()
+        else:
+            for out in self.others():
+                out.start()
+
+    def add(self, into, other):
+        for b in range(into.shape[0]):
+            add_rows(into.at[b], other.at[b], min(16, into.shape[1]))
+
+    def step(self):
+        if self.nf == 4:
+            for h in range(2):
+                _, _, second, at = self.way(h)
+                self.firsts(h)[0].wait_recv()
+                self.add(self.landed.at[3 * h], self.parts.at[second, at])
+                self.second_(h).start()
+
+    def final(self, h):
+        me = lax.axis_index("fsdp")
+        at = pl.ds(h * self.half, self.half)
+        if self.nf == 4:
+            self.firsts(h)[1].wait_recv()
+            into = self.total.at[at]
+            into[...] = self.parts[me, at]
+            self.add(into, self.landed.at[3 * h + 1])
+            self.second_(h).wait_recv()
+            self.add(into, self.landed.at[3 * h + 2])
+        else:
+            into = self.total.at[at]
+            into[...] = self.parts[me, at]
+            for j, out in enumerate(self.others()):
+                if h == 0:
+                    out.wait_recv()
+                self.add(into, self.landed.at[j + 1, at])
+
+    def end(self):
+        if self.nf == 4:
+            for h in range(2):
+                for out in (*self.firsts(h), self.second_(h)):
+                    out.wait_send()
+        else:
+            for out in self.others():
+                out.wait_send()
+
+
+class Exchange:
+    def __init__(self, axis, n, own, every, sems):
+        self.axis, self.n, self.own, self.every = axis, n, own, every
+        self.send, self.got = sems
+
+    def copies(self):
+        me = lax.axis_index(self.axis)
+        for j in range(1, self.n):
+            to, frm = lax.rem(me + j, self.n), lax.rem(me + self.n - j, self.n)
+            args = (self.send.at[j], self.got.at[j], {self.axis: to})
+            yield push(self.own, self.every.at[me], *args), push(self.own, self.every.at[frm], *args)
+
+    def begin(self):
+        self.every[lax.axis_index(self.axis)] = self.own[...]
+        for out, _ in self.copies():
+            out.start()
+
+    def wait(self):
+        for out, arrived in self.copies():
+            arrived.wait_recv()
+            out.wait_send()
+
+    def total(self):
+        result = self.every[0]
+        for i in range(1, self.n):
+            result = result + self.every[i]
+        return result
+
+
+def scatter_kernel(
+    nc, nf, strided, dnormed, gin, gout, small, hidden, cot, gain,
+    d_hidden, pieces, gout_mine, small_all, gain_all,
+    acc, landed, total, in_landed, in_sum, out_landed, out_sum,
+    small_held, small_sum, gain_held, gain_own, gain_sum,
+    line_side, line_sems, in_sems, out_sems, piece_sems, small_sems, here,
+):
+    nz, _, _ = line_of(nc)
+    me_c, me_f = lax.axis_index("ctx"), lax.axis_index("fsdp")
+    line = LineReduce(
+        nc, dnormed, acc, landed,
+        (line_side.at[0], line_side.at[1], line_sems.at[0], line_sems.at[1]),
+    )
+    ins = SquareReduce(nf, gin, in_landed, in_sum, (in_sems.at[0], in_sems.at[1]))
+    outs = SquareReduce(nf, gout, out_landed, out_sum, (out_sems.at[0], out_sems.at[1]))
+    pair = lambda i: (small_sems.at[i, 0], small_sems.at[i, 1])
+    smalls = (
+        Exchange("fsdp", nf, small, small_held, pair(0)),
+        Exchange("ctx", nc, small_sum, small_all, pair(1)),
+    )
+    gains = (
+        Exchange("fsdp", nf, gain_own, gain_held, pair(2)),
+        Exchange("ctx", nc, gain_sum, gain_all, pair(3)),
+    )
+    found = [({"ctx": lax.rem(me_c + j, nc)}, None) for j in range(1, nc)]
+    found += [({"fsdp": lax.rem(me_f + j, nf)}, None) for j in range(1, nf)]
+    if strided:
+        lead, place = me_f * nc + me_c, me_c * nf + me_f
+        target = {"ctx": lead // nf, "fsdp": lax.rem(lead, nf)}
+        source = {"ctx": lax.rem(place, nc), "fsdp": place // nc}
+        away = lead != place
+        found += [(target, away), (source, away)]
+    greet(found)
+
+    ins.begin()
+    line.begin()
+    smalls[0].begin()
+    line.merge()
+    for i in range(nz - 1):
+        line.step(i)
+        if i == 0:
+            smalls[0].wait()
+            small_sum[...] = smalls[0].total()
+            smalls[1].begin()
+    ins.step()
+    outs.begin()
+    line.final(total)
+    gain_own[...] = jnp.zeros_like(gain_own)
+    block = 16
+
+    def norm_back(i, _):
+        at = pl.ds(pl.multiple_of(i * block, block), block)
+        src = hidden[at].astype(F32)
+        dn = total[at]
+        scale = lax.rsqrt(jnp.mean(src * src, axis=1, keepdims=True) + EPS)
+        h = dn * gain[0:1, :]
+        pull = jnp.mean(h * src, axis=1, keepdims=True) * scale * scale
+        d_hidden[at] = scale * (h - src * pull) + cot[at].astype(F32)
+        gain_own[0:1, :] += jnp.sum(dn * src * scale, axis=0, keepdims=True)
+        return 0
+
+    lax.fori_loop(0, hidden.shape[0] // block, norm_back, 0)
+    gains[0].begin()
+
+    def piece(c):
+        return push(
+            in_sum.at[c], pieces.at[me_c], piece_sems.at[0, c], piece_sems.at[1, me_c], {"ctx": c}
+        )
+
+    def piece_from(c):
+        return push(in_sum.at[c], pieces.at[c], piece_sems.at[0, c], piece_sems.at[1, c], {"ctx": c})
+
+    stay = pltpu.make_async_copy(in_sum.at[me_c], pieces.at[me_c], here.at[0])
+    half = nc // 2
+    for h in range(2):
+        ins.final(h)
+        for j in range(half):
+            c = h * half + lax.rem(me_c + j, half)
+            pl.when(c != me_c)(piece(c).start)
+            pl.when(c == me_c)(stay.start)
+    gains[0].wait()
+    gain_sum[...] = gains[0].total()
+    gains[1].begin()
+    outs.step()
+    outs.final(0)
+    outs.final(1)
+    if strided:
+        route = push(out_sum, gout_mine, piece_sems.at[0, nc], piece_sems.at[1, nc], target)
+        pl.when(away)(route.start)
+
+        @pl.when(jnp.logical_not(away))
+        def _():
+            pltpu.make_async_copy(out_sum, gout_mine, here.at[1]).start()
+
+    else:
+        gout_mine[...] = out_sum[...]
+    smalls[1].wait()
+    gains[1].wait()
+    line.end()
+    ins.end()
+    outs.end()
+    stay.wait()
+    for c in range(nc):
+
+        @pl.when(c != me_c)
+        def _():
+            piece_from(c).wait_recv()
+            piece(c).wait_send()
+
+    if strided:
+
+        @pl.when(away)
+        def _():
+            route.wait_recv()
+            route.wait_send()
+
+        @pl.when(jnp.logical_not(away))
+        def _():
+            pltpu.make_async_copy(out_sum, gout_mine, here.at[1]).wait()
+
+
+def call_scatter(nc, nf, strided, dnormed, gin, gout, small, hidden, cot, gain):
+    nz = nc // 2
+    mine = hidden.shape[0]
+    vmem = pl.BlockSpec(memory_space=pltpu.VMEM)
+    dma = pltpu.SemaphoreType.DMA
+    count = max(nf, 6)
+    return pl.pallas_call(
+        functools.partial(scatter_kernel, nc, nf, strided),
+        in_specs=[vmem] * 7,
+        out_specs=[vmem] * 5,
+        out_shape=[
+            jax.ShapeDtypeStruct((mine, D), F32),
+            jax.ShapeDtypeStruct(gin.shape[1:], BF16),
+            jax.ShapeDtypeStruct(gout.shape[1:], BF16),
+            jax.ShapeDtypeStruct((nc,) + small.shape, F32),
+            jax.ShapeDtypeStruct((nc, 8, D), F32),
+        ],
+        scratch_shapes=[
+            pltpu.VMEM((nz, mine, D), BF16),
+            pltpu.VMEM((2, nz, mine, D), BF16),
+            pltpu.VMEM((mine, D), F32),
+            pltpu.VMEM(SquareReduce.landing(nf, gin.shape[1:]), BF16),
+            pltpu.VMEM(gin.shape[1:], BF16),
+            pltpu.VMEM(SquareReduce.landing(nf, gout.shape[1:]), BF16),
+            pltpu.VMEM(gout.shape[1:], BF16),
+            pltpu.VMEM((nf,) + small.shape, F32),
+            pltpu.VMEM(small.shape, F32),
+            pltpu.VMEM((nf, 8, D), F32),
+            pltpu.VMEM((8, D), F32),
+            pltpu.VMEM((8, D), F32),
+            dma((2, nz)),
+            dma((2, 2, nz)),
+            dma((2, count)),
+            dma((2, count)),
+            dma((2, nc + 1)),
+            dma((4, 2, max(nc, nf))),
+            dma((2,)),
+        ],
+        compiler_params=pltpu.CompilerParams(
+            collective_id=2, has_side_effects=True, vmem_limit_bytes=VMEM_LIMIT
+        ),
+        name="scatter",
+    )(dnormed, gin, gout, small, hidden, cot, gain)
+
+
 def rms_scale(values, gain_vec):
     return values * lax.rsqrt(jnp.mean(values * values, axis=-1, keepdims=True) + EPS) * gain_vec
 
@@ -762,14 +1121,8 @@
     g = by_chunk(mixed) * jax.nn.silu(gate)
     gated = (g * by_chunk(scale[..., None]) * chan_par[1]).astype(BF16).reshape(nc * mine, cw)
     branch = dot(gated, out_w).astype(BF16).reshape(nc, mine, D)
+    branch, scales = lax.optimization_barrier((branch, scales))
     out = lax.psum_scatter(branch, "ctx", scatter_dimension=0).astype(F32) + source.reshape(mine, D)
-    grad_out = lax.psum_scatter(
-        dot(gated, cot_all, 0, 0).astype(BF16), "fsdp", scatter_dimension=0, tiled=True
-    )
-    if span > 1:
-        route = [(c * nf + f, f * nc + c) for c in range(nc) for f in range(nf)]
-        grad_out = lax.ppermute(grad_out, ("ctx", "fsdp"), route)
-    grad_out = grad_out.astype(F32)
 
     dproj, dconv, dheads, dchan = call_backward(
         cw, per, seq_lengths, proj, conv_par, heads_par, chan_par, grad_gated, mixed, pre, states,
@@ -777,63 +1130,56 @@
     )
     dproj = dproj.reshape(nc * mine, -1)
     dnormed = dot(dproj, in_w, 1, 1).astype(BF16).reshape(nc, mine, D)
-    dnormed = lax.psum_scatter(dnormed, "ctx", scatter_dimension=0).astype(F32)
-    _, norm_pull = jax.vjp(rms_scale, source, norm_gain)
-    dsource, dnorm_gain = norm_pull(dnormed.reshape(seqs, length, D))
-    d_hidden = dsource + cot.astype(F32).reshape(seqs, length, D)
-
     rows = D // (nc * nf)
-    partial = dot(normed_all, dproj, 0, 0).astype(BF16).reshape(nc, nf, rows, -1)
-    partial = lax.psum_scatter(partial, "fsdp", scatter_dimension=1)
-    pieces = lax.all_to_all(partial, "ctx", split_axis=0, concat_axis=0, tiled=True)
-    side = lambda a: jnp.transpose(
-        a.reshape(nc, rows, span, -1), (1, 2, 0, 3)
-    ).reshape(rows, -1)
+    gin = dot(normed_all, dproj, 0, 0).astype(BF16).reshape(nc, nf, rows, -1)
+    gin = jnp.swapaxes(gin, 0, 1)
+    gout = dot(gated, cot_all, 0, 0).astype(BF16).reshape(nf, 2, wide * span // nf // 2, D)
+    lanes = lambda a: a.reshape(-1, LANES)
+    small = jnp.concatenate(
+        [lanes(dconv[: CONV_K + 1, :cw]), lanes(dchan[0:2]), dheads[0:2], lanes(dconv[: CONV_K + 1, cw:])],
+        axis=0,
+    )
+    small_rows = small.shape[0]
+    small = jnp.pad(small, ((0, -small_rows % 8), (0, 0)))
+    d_hidden, pieces, gout, small_all, gain_all = call_scatter(
+        nc, nf, span > 1, dnormed, gin, gout, small, hidden.reshape(mine, D), cot,
+        jnp.broadcast_to(norm_gain[None], (8, D)),
+    )
+    grad_out = gout.reshape(-1, D).astype(F32)
+
+    def ordered(a):
+        a = jnp.moveaxis(a.reshape(a.shape[:-1] + (span, -1)), 0, -2)
+        return a.reshape(a.shape[:-3] + (-1,))
+
     grad_in = jnp.concatenate(
         [
-            side(pieces[:, :, :cw]),
-            side(pieces[:, :, cw : 2 * cw]),
+            ordered(pieces[:, :, :cw]),
+            ordered(pieces[:, :, cw : 2 * cw]),
             jnp.sum(pieces[:, :, 2 * cw : 2 * cw + 2 * N_STATE].astype(F32), axis=0).astype(BF16),
-            side(pieces[:, :, 2 * cw + 2 * N_STATE : 2 * cw + 2 * N_STATE + heads]),
+            ordered(pieces[:, :, 2 * cw + 2 * N_STATE : 2 * cw + 2 * N_STATE + heads]),
         ],
         axis=1,
     ).astype(F32)
-
-    def place(a, unit):
-        axis, size = a.ndim - 1, wide // unit
-        whole = jnp.zeros(a.shape[:-1] + (DI // unit,), F32)
-        for i in range(span):
-            part = lax.slice_in_dim(a, i * size, (i + 1) * size, axis=axis)
-            whole = lax.dynamic_update_slice_in_dim(
-                whole, part, (i * apart + wide * me_c) // unit, axis
-            )
-        return whole
-
-    dconv = jnp.concatenate(
-        [place(dconv[: CONV_K + 1, :cw], 1), dconv[: CONV_K + 1, cw:]], axis=1
-    )
-    dskip = jnp.sum(dchan[0].reshape(heads, HEAD_DIM), axis=1)
-    small = (
-        dnorm_gain,
-        dconv,
-        place(dheads[0, :heads], HEAD_DIM),
-        place(dheads[1, :heads], HEAD_DIM),
-        place(dskip, HEAD_DIM),
-        place(dchan[1], 1),
-    )
-    dnorm_gain, dconv, dbias, dalog, dskip, dgain = lax.psum(small, ("ctx", "fsdp"))
+    at = 0
+    taken = []
+    for shape in ((CONV_K + 1, cw), (2, cw), (2, LANES), (CONV_K + 1, 2 * N_STATE)):
+        n = shape[0] * shape[1] // LANES
+        taken.append(small_all[:, at : at + n].reshape((nc,) + shape))
+        at += n
+    dconv = jnp.concatenate([ordered(taken[0]), jnp.sum(taken[3], axis=0)], axis=1)
+    dskip = jnp.sum(taken[1][:, 0].reshape(nc, heads, HEAD_DIM), axis=2)
     shape = hidden.shape
     return (
         out.astype(BF16).reshape(shape),
         d_hidden.reshape(shape),
-        dnorm_gain,
+        jnp.sum(gain_all[:, 0], axis=0),
         grad_in,
         dconv[:CONV_K],
         dconv[CONV_K],
-        dbias,
-        dalog,
-        dskip,
-        dgain,
+        ordered(taken[2][:, 0, :heads]),
+        ordered(taken[2][:, 1, :heads]),
+        ordered(dskip),
+        ordered(taken[1][:, 1]),
         grad_out,
     )
 

time: 464 us -> 400 us (0.86)
  waiting for transfers between devices: 153 us -> 0.02 us
  Pallas kernels: 140 us -> 277 us
  blocking collectives: 50.2 us -> 0 us
  local copies, waits for them, and re-layouts: 30.3 us -> 40.4 us
  starting transfers between devices: 9.37 us -> 0.04 us
    pallas_call x0 -> x1, Pallas kernels: none -> 136 us  [call_scatter(): pl.pallas_call(functools.partial(scatter_kernel, nc, nf, strided), in_spe...]
    psum x1 -> x0, waiting for transfers between devices: 84.7 us -> none  [local(): lax.psum(small, ('ctx', 'fsdp'))]
    psum x1 -> x0, blocking collectives: 50.2 us -> none  [local(): lax.psum(small, ('ctx', 'fsdp'))]
    unnamed x6 -> x1, waiting for transfers between devices: 37 us -> 0.02 us
    reduce_scatter x2 -> x0, waiting for transfers between devices: 31 us -> none  [the longest x1 31 us: local(): lax.psum_scatter(dot(gated, cot_all, 0, 0).astype(BF16), 'fsdp', scatter_...]
    slice x2 -> x11, local copies, waits for them, and re-layouts: 0.91 us -> 6.76 us  [the longest x3 1.88 us: local(): taken.append(small_all[:, at:at + n].reshape((nc,) + shape))]
    all_to_all x1 -> x0, starting transfers between devices: 5.36 us -> none  [local(): lax.all_to_all(partial, 'ctx', split_axis=0, concat_axis=0, tiled=True)]
    unnamed x57 -> x55, local copies, waits for them, and re-layouts: 6.09 us -> 10.4 us
  transfers between devices with their start and end apart: 7 -> 1, of which waited for: 3 -> 0; matrix products, arithmetic and copies ran while one was open for 8% -> 13% of each run, Pallas kernels for 0% -> 41%
where the time goes in v3:
time: 400 us; the launch traced here: 394 us
  Pallas kernels  277 us (69%)
  matrix products  45.5 us (11%)
  local copies, waits for them, and re-layouts  40.4 us (10%)
  other arithmetic  16.7 us (4%)
  between operations  14.6 us (4%)
    pallas_call x1, Pallas kernels, call_scatter(): pl.pallas_call(functools.partial(scatter_kernel, nc, nf, strided), in_spe...  136 us
    pallas_call x1, Pallas kernels, call_gather(): pl.pallas_call(functools.partial(gather_kernel, nc, nf, spread), in_specs...  95.1 us
    dot_general x6, matrix products, dot(): lax.dot_general(a.astype(BF16), b.astype(BF16), (((ca,), (cb,)), ((), ())...  45.5 us
    pallas_call x1, Pallas kernels, call_backward(): pl.pallas_call(functools.partial(backward_kernel, cw, chunks), grid=(chun...  23.3 us
    pallas_call x1, Pallas kernels, call_forward(): pl.pallas_call(functools.partial(forward_kernel, cw), grid=(chunks,), in_...  13.8 us
    unnamed x55, local copies, waits for them, and re-layouts  10.4 us
    pallas_call x1, Pallas kernels, add_over_ctx(): pl.pallas_call(functools.partial(add_over_ctx_kernel, nc), in_specs=[pl.B...  8.12 us
  transfers between devices with their start and end apart: 1, of which 0 were waited for; matrix products, arithmetic and copies ran while one was open for 13% of the time, Pallas kernels for 41%

profile of v3, /device:TPU:1, one launch (start us, length us, event | category | flops | bytes accessed | tf_op | source)
XLA Modules:
  0.0 394.0 jit_solution(7317916946683028063)
XLA Ops:
  7.4 1.2 multiply_reduce_fusion
  20.3 1.4 constant_dynamic-slice_fusion.9
  26.0 1.9 constant_dynamic-slice_fusion.4.out_rows
  28.2 1.1 copy-done.2
  29.3 95.1 %gather.1 = (bf16[8,128,2048]{2,1,0:T(8,128)(2,1)}, bf16[8,128,2048]{2,1,0:T(8,128)(2,1)}, bf16[4,512,1408]{2,1,0:T(8,128)(2,1)}, bf16[4,128,2048]{2,1,0:T(8,128)(2,1)}) custom-call(bf16[128,2048]{1,0:T(8,128)(2,1)} %fusion.9.normed, bf16[128,2048]{1,0:T(8,128)(2,1)} %bitcast.117, bf16[512,1408]{1,0:T(8,128)(2,1)} %copy-done.2, ...), custom_call_target="tpu_custom_call" | custom-call | tf_op jit(solution)/shard_map/gather/pallas_call | solution.py:601
  124.5 6.7 %fusion.22.grad_gated = f32[8,2,64,512]{3,2,1,0:T(8,128)} fusion(bf16[8,2,64,2048]{3,2,1,0:T(8,128)(2,1)} %bitcast.143, bf16[512,2048,1,1]{1,0,3,2:T(8,128)(2,1)} %bitcast.149), kind=kOutput, calls=%fused_computation.101 | convolution fusion | flops 2147483648 | bytes 8388608 | tf_op jit(solution)/shard_map/dot_general | solution.py:26
  131.1 7.9 %convolution_convert_fusion.1 = bf16[1024,1408]{1,0:T(8,128)(2,1)} fusion(bf16[1024,2048]{1,0:T(8,128)(2,1)S(1)} %bitcast.146, bf16[2048,1408]{1,0:T(8,128)(2,1)S(1)} %bitcast.142), kind=kOutput, calls=%fused_computation.2 | convolution fusion | flops 5907021824 | bytes 12845056 | tf_op jit(solution)/shard_map/dot_general | solution.py:26
  139.8 13.8 %mixer_forward.1 = (f32[4,2,128,512]{3,2,1,0:T(8,128)}, f32[4,2,128,768]{3,2,1,0:T(8,128)}, f32[4,2,128,512]{3,2,1,0:T(8,128)}, f32[4,2,8,128]{3,2,1,0:T(8,128)}) custom-call(s32[2]{0:T(128)} %bitcast.139, bf16[8,2,64,1408]{3,2,1,0:T(8,128)(2,1)} %bitcast.107, f32[8,768]{1,0:T(8,128)} %maximum_maximum_fusion.conv_w, ...), custom_call_target="tpu_custom_call" | custom-call | tf_op jit(solution)/shard_map/mixer_forward/pallas_call | solution.py:265
  153.6 1.4 slice.90
  155.0 8.1 %add_over_ctx.1 = f32[16,128]{1,0:T(8,128)} custom-call(f32[16,128]{1,0:T(8,128)} %bitcast.132), custom_call_target="tpu_custom_call" | custom-call | tf_op jit(solution)/shard_map/add_over_ctx/pallas_call | solution.py:640
  165.7 1.7 fusion.14
  167.7 2.1 fusion.6
  169.8 4.3 %convolution_convert_fusion.3 = bf16[1024,2048]{1,0:T(8,128)(2,1)} fusion(bf16[1024,512]{1,0:T(8,128)(2,1)S(1)} %bitcast.125, bf16[512,2048]{1,0:T(8,128)(2,1)S(1)} %bitcast.150), kind=kOutput, calls=%fused_computation.4 | convolution fusion | flops 2149580800 | bytes 7340032 | tf_op jit(solution)/shard_map/dot_general | solution.py:26
  174.2 23.3 %mixer_backward.1 = (bf16[8,2,64,1408]{3,2,1,0:T(8,128)(2,1)}, f32[8,768]{1,0:T(8,128)}, f32[8,128]{1,0:T(8,128)}, f32[8,512]{1,0:T(8,128)}) custom-call(s32[2]{0:T(128)} %bitcast.140, bf16[8,2,64,1408]{3,2,1,0:T(8,128)(2,1)} %bitcast.109, f32[8,768]{1,0:T(8,128)} %maximum_maximum_fusion.conv_w, f32[8,128]{1,0:T(8,128)} %maximum_maximum_fusion.2.heads_par, ...), custom_call_target="tpu_custom_call" | custom-call | tf_op jit(solution)/shard_map/mixer_backward/pallas_call | solution.py:307
  198.9 9.5 %convolution_convert_fusion = bf16[2048,1408]{1,0:T(8,128)(2,1)S(1)} fusion(bf16[1024,2048]{1,0:T(8,128)(2,1)} %bitcast.145, bf16[1024,1408]{1,0:T(8,128)(2,1)} %bitcast.147), kind=kOutput, calls=%fused_computation | convolution fusion | flops 5908463616 | bytes 12845056 | tf_op jit(solution)/shard_map/dot_general | solution.py:26
  208.4 2.9 copy.149
  213.4 6.1 %convolution_convert_fusion.4 = bf16[512,2048]{1,0:T(8,128)(2,1)} fusion(bf16[1024,512]{1,0:T(8,128)(2,1)S(1)} %bitcast.126, bf16[1024,2048]{1,0:T(8,128)(2,1)} %bitcast.144), kind=kOutput, calls=%fused_computation.5 | convolution fusion | flops 2148532224 | bytes 7340032 | tf_op jit(solution)/shard_map/dot_general | solution.py:26
  219.5 10.9 %convolution_convert_fusion.2 = bf16[1024,2048]{1,0:T(8,128)(2,1)} fusion(bf16[1024,1408]{1,0:T(8,128)(2,1)S(1)} %bitcast.148, bf16[2048,1408]{1,0:T(8,128)(2,1)} %bitcast.141), kind=kOutput, calls=%fused_computation.3 | convolution fusion | flops 5907677184 | bytes 12845056 | tf_op jit(solution)/shard_map/dot_general | solution.py:26
  231.1 136.5 %scatter.1 = (f32[128,2048]{1,0:T(8,128)}, bf16[8,64,1408]{2,1,0:T(8,128)(2,1)}, bf16[2,64,2048]{2,1,0:T(8,128)(2,1)}, f32[8,40,128]{2,1,0:T(8,128)}, f32[8,8,2048]{2,1,0:T(8,128)}) custom-call(bf16[8,128,2048]{2,1,0:T(8,128)(2,1)} %bitcast.113, bf16[4,8,64,1408]{3,2,1,0:T(8,128)(2,1)} %bitcast.106, bf16[4,2,64,2048]{3,2,1,0:T(8,128)(2,1)} %bitcast.123, ...), custom_call_target="tpu_custom_call" | custom-call | tf_op jit(solution)/shard_map/scatter/pallas_call | solution.py:975
  378.3 1.6 slice_reduce_fusion.3
  379.9 1.7 slice_reduce_fusion.2
  381.6 1.1 bitcast_convert_fusion
  382.8 1.5 maximum_convert_fusion
  384.3 2.0 fusion.7
  (134 shorter events, 35.6 us)
Async XLA Ops:
  7.2 377.1 %reduce-scatter.2.cloned.1.call-start = ((), (), s32[]{:S(2)}) async-start(), calls=%async_computation.1 | async-start | bytes 4718592 | tf_op jit(solution)/shard_map/reduce_scatter | solution.py:1125
  20.2 4.8 %copy-start = (bf16[2,1,64,2048]{3,2,1,0:T(8,128)(2,1)S(1)}, bf16[2,1,64,2048]{3,2,1,0:T(8,128)(2,1)}, u32[]{:S(2)}) copy-start(bf16[2,1,64,2048]{3,2,1,0:T(8,128)(2,1)} %param.12) | copy-start | bytes 1572868
  20.3 4.7 %copy-start.7 = (f32[2048]{0:T(1024)S(1)}, f32[2048]{0:T(1024)}, u32[]{:S(2)}) copy-start(f32[2048]{0:T(1024)} %param.15) | copy-start | bytes 24580
  28.2 1.1 copy-start.2
  124.4 6.7 %copy-start.8 = (bf16[4,512,1408]{2,1,0:T(8,128)(2,1)S(1)}, bf16[4,512,1408]{2,1,0:T(8,128)(2,1)}, u32[]{:S(2)}) copy-start(bf16[4,512,1408]{2,1,0:T(8,128)(2,1)} %get-tuple-element.31) | copy-start | bytes 17301508
  124.4 6.7 %copy-start.9 = (bf16[8,128,2048]{2,1,0:T(8,128)(2,1)S(1)}, bf16[8,128,2048]{2,1,0:T(8,128)(2,1)}, u32[]{:S(2)}) copy-start(bf16[8,128,2048]{2,1,0:T(8,128)(2,1)} %get-tuple-element.30) | copy-start | bytes 12582916
  167.7 2.1 copy-start.11
  213.4 6.1 %copy-start.10 = (bf16[8,2,64,1408]{3,2,1,0:T(8,128)(2,1)S(1)}, bf16[8,2,64,1408]{3,2,1,0:T(8,128)(2,1)}, u32[]{:S(2)}) copy-start(bf16[8,2,64,1408]{3,2,1,0:T(8,128)(2,1)} %get-tuple-element.40) | copy-start | bytes 8650756
  367.5 8.7 %copy-start.3 = (bf16[8,64,1408]{2,1,0:T(8,128)(2,1)S(1)}, bf16[8,64,1408]{2,1,0:T(8,128)(2,1)}, u32[]{:S(2)}) copy-start(bf16[8,64,1408]{2,1,0:T(8,128)(2,1)} %get-tuple-element.46) | copy-start | bytes 4325380
  374.4 0.7 copy-start.6
  377.1 4.5 %copy-start.5 = (bf16[2,64,2048]{2,1,0:T(8,128)(2,1)S(1)}, bf16[2,64,2048]{2,1,0:T(8,128)(2,1)}, u32[]{:S(2)}) copy-start(bf16[2,64,2048]{2,1,0:T(8,128)(2,1)} %get-tuple-element.48) | copy-start | bytes 1572868
  381.6 2.6 copy-start.1
  382.7 3.5 copy-start.4
Sparse Core Ops, SparseCore 0:
  174.3 47.4 reduce-scatter.1

commit v4 on v3

--- a/solution.py
+++ b/solution.py
@@ -79,76 +79,61 @@
     return z, step, cum
 
 
-def forward_kernel(
-    cw, lengths, proj, conv_w, heads_par, chan_par, grad_gated, mixed_out, pre_out, state_out,
-    stats_out, window, state,
-):
-    chunk = pl.program_id(0)
-    seqs = proj.shape[1]
-    q = proj.shape[0] * proj.shape[2]
+def head_pick(cw, span, me_c):
+    mine, apart, each = cw // HEAD_DIM, HEADS // span, cw // HEAD_DIM // span
+    lane = lax.broadcasted_iota(jnp.int32, (LANES, LANES), 1)
+    head = (lane // each) * apart + me_c * each + lax.rem(lane, each)
+    row = lax.broadcasted_iota(jnp.int32, (LANES, LANES), 0)
+    return jnp.logical_and(row == head, lane < mine).astype(F32)
+
+
+def forward_chunk(cw, chunk, s, lengths, proj, pick, conv_w, heads_par, chan_par, mixed_out, pre_out, state_out, window, state):
+    per = 2 if proj.shape[0] % 2 == 0 else 1
+    length = proj.shape[2]
+    q = per * length
     cc = cw + 2 * N_STATE
     causal = triangle(q, True)
-
-    @pl.when(chunk == 0)
-    def _():
-        window[...] = jnp.zeros_like(window)
-        state[...] = jnp.zeros_like(state)
-
-    for s in range(seqs):
-        rows = proj[:, s].reshape(q, proj.shape[3])
-        gate = rows[:, :cw].astype(F32)
-        window[s, 8 : 8 + q, :] = rows[:, cw : cw + cc].astype(F32)
-        pre = conv_w[CONV_K : CONV_K + 1, :] + conv_w[0:1, :] * window[s, 5 : 5 + q, :]
-        for k in range(1, CONV_K):
-            pre = pre + conv_w[k : k + 1, :] * window[s, 5 + k : 5 + k + q, :]
-        window[s, 0:8, :] = window[s, q : q + 8, :]
-        pre_out[0, s] = pre
-        act = pre * jax.nn.sigmoid(pre)
-        x = act[:, :cw]
-        b = act[:, cw : cw + N_STATE]
-        c = act[:, cw + N_STATE :]
-        live = live_column(lengths, s, chunk, q)
-        _, step, cum = decays(
-            rows[:, cw + cc :].astype(F32), heads_par[0:1, :], heads_par[1:2, :], live
-        )
-        cum_t = cum.T
-        last = cum[q - 1 : q, :]
-        u = x * to_lanes(step, cw)
-        gram = dot(c, b, 1, 1)
-        within = []
-        for j in range(cw // LANES):
-            kernels = []
-            for h in (2 * j, 2 * j + 1):
-                spread = jnp.where(causal, cum[:, h : h + 1] - cum_t[h : h + 1, :], -1e30)
-                kernels.append((gram * jnp.exp(spread)).astype(BF16))
-            both = jnp.concatenate(kernels, axis=1)
-            within.append(dot(both, split_heads(u[:, j * LANES : (j + 1) * LANES])))
-        before = state[s]
-        state_out[0, s] = before
-        mixed = (
-            jnp.concatenate(within, axis=1)
-            + dot(c, before) * to_lanes(jnp.exp(cum), cw)
-            + chan_par[0:1, :] * x
-        )
-        mixed_out[0, s] = mixed
-        left = to_lanes(jnp.exp(last - cum), cw)
-        state[s] = before * to_lanes(jnp.exp(last), cw) + dot(b, left * u, 0, 0)
-        g = mixed * gate * jax.nn.sigmoid(gate)
-        gg = grad_gated[:, s].reshape(q, cw)
-        ones = jnp.ones((8, cw), F32)
-        first = lax.dot_general(
-            ones, g * g, (((1,), (1,)), ((), ())), precision=EXACT, preferred_element_type=F32
-        )
-        second = lax.dot_general(
-            ones, gg * chan_par[1:2, :] * g, (((1,), (1,)), ((), ())), precision=EXACT,
-            preferred_element_type=F32,
-        )
-        stats_out[0, s, 0:1, :] = first[0:1, :]
-        stats_out[0, s, 1:2, :] = second[0:1, :]
+    at = pl.ds(chunk * per, per)
+    rows = proj[at, s].reshape(q, proj.shape[3])
+    window[s, 8 : 8 + q, :] = rows[:, cw : cw + cc].astype(F32)
+    pre = conv_w[CONV_K : CONV_K + 1, :] + conv_w[0:1, :] * window[s, 5 : 5 + q, :]
+    for k in range(1, CONV_K):
+        pre = pre + conv_w[k : k + 1, :] * window[s, 5 + k : 5 + k + q, :]
+    window[s, 0:8, :] = window[s, q : q + 8, :]
+    pre_out[chunk, s] = pre
+    act = pre * jax.nn.sigmoid(pre)
+    x = act[:, :cw]
+    b = act[:, cw : cw + N_STATE]
+    c = act[:, cw + N_STATE :]
+    live = live_column(lengths, s, chunk, q)
+    _, step, cum = decays(
+        dot(rows[:, cw + cc :], pick[...]), heads_par[0:1, :], heads_par[1:2, :], live
+    )
+    cum_t = cum.T
+    last = cum[q - 1 : q, :]
+    u = x * to_lanes(step, cw)
+    gram = dot(c, b, 1, 1)
+    within = []
+    for j in range(cw // LANES):
+        kernels = []
+        for h in (2 * j, 2 * j + 1):
+            spread = jnp.where(causal, cum[:, h : h + 1] - cum_t[h : h + 1, :], -1e30)
+            kernels.append((gram * jnp.exp(spread)).astype(BF16))
+        both = jnp.concatenate(kernels, axis=1)
+        within.append(dot(both, split_heads(u[:, j * LANES : (j + 1) * LANES])))
+    before = state[s]
+    state_out[chunk, s] = before
+    mixed_out[chunk, s] = (
+        jnp.concatenate(within, axis=1)
+        + dot(c, before) * to_lanes(jnp.exp(cum), cw)
+        + chan_par[0:1, :] * x
+    )
+    left = to_lanes(jnp.exp(last - cum), cw)
+    state[s] = before * to_lanes(jnp.exp(last), cw) + dot(b, left * u, 0, 0)
 
 
 def backward_kernel(
-    cw, chunks, lengths, proj, conv_w, heads_par, chan_par, grad_gated, mixed_in, pre_in, state_in,
+    cw, chunks, lengths, proj, pick, conv_w, heads_par, chan_par, grad_gated, mixed_in, pre_in, state_in,
     scale_in, dproj_out, dconv_out, dheads_out, dchan_out, window, state_grad,
 ):
     step_id = pl.program_id(0)
@@ -195,7 +180,7 @@
         c = act[:, cw + N_STATE :]
         live = live_column(lengths, s, chunk, q)
         z, step, cum = decays(
-            rows[:, cw + cc :].astype(F32), heads_par[0:1, :], heads_par[1:2, :], live
+            dot(rows[:, cw + cc :], pick[...]), heads_par[0:1, :], heads_par[1:2, :], live
         )
         cum_t = cum.T
         last = cum[q - 1 : q, :]
@@ -253,49 +238,12 @@
         window[s, q : q + 8, :] = window[s, 0:8, :]
         dproj_out[:, s, :, :cw] = dgate.astype(BF16).reshape(blocks, q // blocks, cw)
         dproj_out[:, s, :, cw : cw + cc] = dconv_in.astype(BF16).reshape(blocks, q // blocks, cc)
-        dproj_out[:, s, :, cw + cc :] = dz.astype(BF16).reshape(blocks, q // blocks, LANES)
-
-
-def call_forward(cw, per, lengths, proj, conv_w, heads_par, chan_par, grad_gated):
-    nc, seqs, length, cols = proj.shape
-    chunks, q, cc = nc // per, per * length, cw + 2 * N_STATE
-    whole = lambda a: pl.BlockSpec(a.shape, lambda i: (0,) * a.ndim)
-    by_chunk = lambda n: pl.BlockSpec((1, seqs, n[0], n[1]), lambda i: (i, 0, 0, 0))
-    tokens = lambda n: pl.BlockSpec((per, seqs, length, n), lambda i: (i, 0, 0, 0))
-    return pl.pallas_call(
-        functools.partial(forward_kernel, cw),
-        grid=(chunks,),
-        in_specs=[
-            pl.BlockSpec(memory_space=pltpu.SMEM),
-            tokens(cols),
-            whole(conv_w),
-            whole(heads_par),
-            whole(chan_par),
-            tokens(cw),
-        ],
-        out_specs=[
-            by_chunk((q, cw)),
-            by_chunk((q, cc)),
-            by_chunk((N_STATE, cw)),
-            by_chunk((8, q)),
-        ],
-        out_shape=[
-            jax.ShapeDtypeStruct((chunks, seqs, q, cw), F32),
-            jax.ShapeDtypeStruct((chunks, seqs, q, cc), F32),
-            jax.ShapeDtypeStruct((chunks, seqs, N_STATE, cw), F32),
-            jax.ShapeDtypeStruct((chunks, seqs, 8, q), F32),
-        ],
-        scratch_shapes=[
-            pltpu.VMEM((seqs, q + 8, cc), F32),
-            pltpu.VMEM((seqs, N_STATE, cw), F32),
-        ],
-        compiler_params=pltpu.CompilerParams(vmem_limit_bytes=VMEM_LIMIT),
-        name="mixer_forward",
-    )(lengths, proj, conv_w, heads_par, chan_par, grad_gated)
+        dz = dot(dz, pick[...], 1, 1).astype(BF16)
+        dproj_out[:, s, :, cw + cc :] = dz.reshape(blocks, q // blocks, LANES)
 
 
 def call_backward(
-    cw, per, lengths, proj, conv_w, heads_par, chan_par, grad_gated, mixed, pre, states, scales
+    cw, per, lengths, proj, pick, conv_w, heads_par, chan_par, grad_gated, mixed, pre, states, scales
 ):
     nc, seqs, length, cols = proj.shape
     chunks, q, cc = nc // per, per * length, cw + 2 * N_STATE
@@ -310,6 +258,7 @@
         in_specs=[
             pl.BlockSpec(memory_space=pltpu.SMEM),
             tokens(cols),
+            whole(pick.shape),
             whole(conv_w.shape),
             whole(heads_par.shape),
             whole(chan_par.shape),
@@ -337,7 +286,7 @@
         ],
         compiler_params=pltpu.CompilerParams(vmem_limit_bytes=VMEM_LIMIT),
         name="mixer_backward",
-    )(lengths, proj, conv_w, heads_par, chan_par, grad_gated, mixed, pre, states, scales)
+    )(lengths, proj, pick, conv_w, heads_par, chan_par, grad_gated, mixed, pre, states, scales)
 
 
 MESH = pl.DeviceIdType.MESH
@@ -374,7 +323,7 @@
                 pl.semaphore_signal(barrier, inc=1, device_id=device, device_id_type=MESH)
 
             count = count + there.astype(jnp.int32)
-    pl.semaphore_wait(barrier, count)
+    return lambda: pl.semaphore_wait(barrier, count)
 
 
 def line_of(nc):
@@ -388,117 +337,102 @@
     return me, high * 2 + (1 - low), (1 - high) * 2 + low
 
 
-def gather_neighbours(nc, nf):
-    nz, z, k = line_of(nc)
-    me_f = lax.axis_index("fsdp")
-    found = [
-        ({"ctx": 2 * z + 1 - k}, None),
-        ({"ctx": 2 * (z + 1) + k}, z < nz - 1),
-        ({"ctx": 2 * (z - 1) + k}, z > 0),
-    ]
-    if nf == 4:
-        _, fx, fy = square_partners()
-        found += [({"fsdp": fx}, None), ({"fsdp": fy}, None)]
-    else:
-        found += [({"fsdp": lax.rem(me_f + j, nf)}, None) for j in range(1, nf)]
-    return found
-
-
 class LineGather:
-    def __init__(self, nc, own, every, sems):
+    def __init__(self, nc, every, sems):
         self.nz, self.z, self.k = line_of(nc)
-        self.own, self.every = own, every
-        self.up, self.down, self.side, self.got, self.got_side, self.here = sems
-
-    def slot(self, place, core=None):
-        return self.every.at[2 * place + (self.k if core is None else core)]
+        self.every = every
+        self.up, self.down, self.side, self.got, self.got_side = sems
+
+    def slot(self, place):
+        return self.every.at[2 * place + self.k]
 
     def copies(self, d, below):
         z, k = self.z, self.k
         origin = z - d if below else z + d
-        src = self.own if d == 0 else self.slot(origin)
         to = z + 1 if below else z - 1
         on = push(
-            src, self.slot(origin), (self.up if below else self.down).at[d], self.got.at[origin],
-            {"ctx": 2 * to + k},
+            self.slot(origin), self.slot(origin), (self.up if below else self.down).at[d],
+            self.got.at[origin], {"ctx": 2 * to + k},
         )
         side = push(
-            src, self.slot(origin), self.side.at[origin], self.got_side.at[origin],
+            self.slot(origin), self.slot(origin), self.side.at[origin], self.got_side.at[origin],
             {"ctx": 2 * z + 1 - k},
         )
         there = origin >= 0 if below else origin <= self.nz - 1
         further = to <= self.nz - 1 if below else to >= 0
-        return origin, on, side, there, further
+        return on, side, there, further
 
     def begin(self):
-        pltpu.make_async_copy(self.own, self.slot(self.z), self.here).start()
         for below in (True, False):
-            _, on, side, _, further = self.copies(0, below)
+            on, side, _, further = self.copies(0, below)
             pl.when(further)(on.start)
         side.start()
 
     def step(self, d):
         for below in (True, False):
-            origin, on, side, there, further = self.copies(d, below)
+            on, side, there, further = self.copies(d, below)
 
             @pl.when(there)
             def _():
                 on.wait_recv()
+                pl.when(further)(on.start)
                 side.start()
-                pl.when(further)(on.start)
+
+    def sides(self):
+        for place in range(self.nz):
+            arrived = self.every.at[2 * place + 1 - self.k]
+            push(
+                arrived, arrived, self.side.at[place], self.got_side.at[place],
+                {"ctx": 2 * self.z + 1 - self.k},
+            ).wait_recv()
 
     def end(self):
-        z, k, nz = self.z, self.k, self.nz
-        pltpu.make_async_copy(self.own, self.slot(z), self.here).wait()
-        for place in range(nz):
-            arrived = self.every.at[2 * place + 1 - k]
+        for place in range(self.nz):
+            arrived = self.every.at[2 * place + 1 - self.k]
             push(
-                arrived, arrived, self.side.at[place], self.got_side.at[place], {"ctx": 2 * z + 1 - k}
-            ).wait()
-        for d in range(nz - 1):
+                arrived, arrived, self.side.at[place], self.got_side.at[place],
+                {"ctx": 2 * self.z + 1 - self.k},
+            ).wait_send()
+        for d in range(self.nz - 1):
             for below in (True, False):
-                _, on, _, there, further = self.copies(d, below)
+                on, _, there, further = self.copies(d, below)
                 pl.when(jnp.logical_and(there, further))(on.wait_send)
 
 
 class SquareGather:
-    def __init__(self, nf, own, every, sems):
-        self.nf, self.own, self.every = nf, own, every
-        self.send, self.got, self.here = sems
-        self.half = own.shape[0] // 2
-
-    def first(self):
+    def __init__(self, nf, every, sems):
+        self.nf, self.every = nf, every
+        self.send, self.got = sems
+        self.half = every.shape[1] // 2
+
+    def peers(self):
         me = lax.axis_index("fsdp")
         if self.nf == 4:
             _, fx, fy = square_partners()
-            peers = [(fx, fx), (fy, fy)]
-        else:
-            peers = [
-                (lax.rem(me + j, self.nf), lax.rem(me + self.nf - j, self.nf))
-                for j in range(1, self.nf)
-            ]
+            return [(fx, fx), (fy, fy)]
         return [
-            (
-                push(self.own, self.every.at[me], self.send.at[j], self.got.at[j], {"fsdp": to}),
-                push(self.own, self.every.at[frm], self.send.at[j], self.got.at[j], {"fsdp": to}),
-            )
-            for j, (to, frm) in enumerate(peers)
+            (lax.rem(me + j, self.nf), lax.rem(me + self.nf - j, self.nf))
+            for j in range(1, self.nf)
         ]
+
+    def first(self):
+        me = lax.axis_index("fsdp")
+        for j, (to, frm) in enumerate(self.peers()):
+            args = (self.send.at[j], self.got.at[j], {"fsdp": to})
+            mine, theirs = self.every.at[me], self.every.at[frm]
+            yield push(mine, mine, *args), push(theirs, theirs, *args)
 
     def second(self):
         me, fx, fy = square_partners()
-        far = 3 - me
         pairs = []
         for j, (via, to) in enumerate(((fx, fy), (fy, fx))):
             rows = pl.ds(j * self.half, self.half)
             args = (self.send.at[2 + j], self.got.at[2 + j], {"fsdp": to})
-            there, here = self.every.at[via, rows], self.every.at[far, rows]
+            there, here = self.every.at[via, rows], self.every.at[3 - me, rows]
             pairs.append((push(there, there, *args), push(here, here, *args)))
         return pairs
 
     def begin(self):
-        me = lax.axis_index("fsdp")
-        pltpu.make_async_copy(self.own, self.every.at[me], self.here).start()
         for out, _ in self.first():
             out.start()
 
@@ -508,148 +442,345 @@
             if self.nf == 4:
                 self.second()[j][0].start()
 
+    def far(self):
+        if self.nf == 4:
+            for _, arrived in self.second():
+                arrived.wait_recv()
+
     def end(self):
-        me = lax.axis_index("fsdp")
-        pltpu.make_async_copy(self.own, self.every.at[me], self.here).wait()
         for out, _ in self.first():
             out.wait_send()
         if self.nf == 4:
-            for out, arrived in self.second():
-                arrived.wait_recv()
+            for out, _ in self.second():
                 out.wait_send()
 
 
-class Spread:
-    def __init__(self, nf, source, own, every, sems):
-        self.nf, self.source, self.own, self.every = nf, source, own, every
-        self.send, self.got, self.here = sems
+class SquareSpread:
+    def __init__(self, nf, source, every, sems):
+        self.nf, self.every = nf, every
+        self.send, self.got = sems
         self.mine = lax.axis_index("fsdp") == source
 
     def copies(self):
         me = lax.axis_index("fsdp")
         return [
             push(
-                self.own, self.every, self.send.at[j], self.got.at[0], {"fsdp": lax.rem(me + j, self.nf)}
+                self.every, self.every, self.send.at[j], self.got.at[0],
+                {"fsdp": lax.rem(me + j, self.nf)},
             )
             for j in range(1, self.nf)
         ]
 
     def begin(self):
-        @pl.when(self.mine)
-        def _():
-            pltpu.make_async_copy(self.own, self.every, self.here).start()
-            for out in self.copies():
-                out.start()
+        for out in self.copies():
+            pl.when(self.mine)(out.start)
 
     def step(self):
         pass
 
+    def far(self):
+        if self.nf > 1:
+            pl.when(jnp.logical_not(self.mine))(self.copies()[0].wait_recv)
+
     def end(self):
-        @pl.when(self.mine)
-        def _():
-            pltpu.make_async_copy(self.own, self.every, self.here).wait()
-            for out in self.copies():
-                out.wait_send()
-
-        if self.nf > 1:
-
-            @pl.when(jnp.logical_not(self.mine))
-            def _():
-                self.copies()[0].wait_recv()
-
-
-def gather_kernel(
-    nc, nf, spread, normed, cot, in_rows, out_rows, normed_all, cot_all, in_all, out_all,
-    line_sems, in_sems, out_sems, here,
+        for out in self.copies():
+            pl.when(self.mine)(out.wait_send)
+
+
+class Exchange:
+    def __init__(self, axis, n, own, every, sems):
+        self.axis, self.n, self.own, self.every = axis, n, own, every
+        self.send, self.got = sems
+
+    def copies(self):
+        me = lax.axis_index(self.axis)
+        for j in range(1, self.n):
+            to, frm = lax.rem(me + j, self.n), lax.rem(me + self.n - j, self.n)
+            args = (self.send.at[j], self.got.at[j], {self.axis: to})
+            yield push(self.own, self.every.at[me], *args), push(self.own, self.every.at[frm], *args)
+
+    def begin(self):
+        self.every[lax.axis_index(self.axis)] = self.own[...]
+        for out, _ in self.copies():
+            out.start()
+
+    def wait(self):
+        for out, arrived in self.copies():
+            arrived.wait_recv()
+            out.wait_send()
+
+    def total(self):
+        result = self.every[0]
+        for i in range(1, self.n):
+            result = result + self.every[i]
+        return result
+
+
+def front_kernel(
+    nc, nf, cw, span, lengths, hidden, cot, in_w, tail, out_w, norm_gain, conv_w, conv_b, heads_in, gate_gain,
+    normed_out, cot_out, main_out, tail_out, rows_out, proj_out, gg_out, mixed_out, pre_out, states_out,
+    scales, conv_par, heads_par, chan_par, pick,
+    normed_v, cot_v, main_v, tail_v, rows_v, acc, proj, gg, mixed, pre, states, window, state,
+    stats, stats_held,
+    line_sems, main_sems, tail_sems, rows_sems, stat_sems, load_sems, keep_sems,
 ):
+    nz, z, k = line_of(nc)
+    me_c, me_f = lax.axis_index("ctx"), lax.axis_index("fsdp")
+    wide, apart = cw // span, DI // span
+    depth = in_w.shape[0]
+    seqs, length = proj.shape[1], proj.shape[2]
+    per = 2 if nc % 2 == 0 else 1
+    q, chunks = per * length, nc // per
+
+    found = [({"ctx": lax.rem(me_c + j, nc)}, None) for j in range(1, nc)]
+    found += [({"fsdp": lax.rem(me_f + j, nf)}, None) for j in range(1, nf)]
+    met = greet(found)
+
+    loads = []
+
+    def load(src, dst):
+        copy = pltpu.make_async_copy(src, dst, load_sems.at[len(loads)])
+        copy.start()
+        loads.append(copy)
+
+    for part in range(2):
+        for i in range(span):
+            start = pl.multiple_of(part * DI + i * apart + wide * me_c, LANES)
+            load(
+                in_w.at[:, pl.ds(start, wide)],
+                main_v.at[me_f, :, pl.ds(part * cw + i * wide, wide)],
+            )
+    load(tail, tail_v.at[me_f])
+    weight_loads = len(loads)
+    load(cot, cot_v.at[me_c])
+    if span > 1:
+        load(out_w.at[pl.ds(pl.multiple_of(wide * me_c, 16), wide)], rows_v.at[me_f])
+    else:
+        lap = out_w.shape[0] // cw
+        held = me_f == me_c // lap
+        rows_load = pltpu.make_async_copy(
+            out_w.at[pl.ds(pl.multiple_of(cw * lax.rem(me_c, lap), 16), cw)], rows_v.at[0],
+            load_sems.at[len(loads)],
+        )
+        pl.when(held)(rows_load.start)
+
+    def norm(i, _):
+        at = pl.ds(pl.multiple_of(i * 16, 16), 16)
+        src = hidden[at].astype(F32)
+        mean = jnp.mean(src * src, axis=1, keepdims=True)
+        normed_v[me_c, at] = (src * lax.rsqrt(mean + EPS) * norm_gain[...]).astype(BF16)
+        return 0
+
+    lax.fori_loop(0, hidden.shape[0] // 16, norm, 0)
+
+    line = lambda i, every: LineGather(nc, every, [line_sems.at[i, j] for j in range(5)])
+    normed_line, cot_line = line(0, normed_v), line(1, cot_v)
+    main = SquareGather(nf, main_v, (main_sems.at[0], main_sems.at[1]))
+    tails = SquareGather(nf, tail_v, (tail_sems.at[0], tail_sems.at[1]))
+    if span > 1:
+        rows = SquareGather(nf, rows_v, (rows_sems.at[0], rows_sems.at[1]))
+    else:
+        rows = SquareSpread(nf, me_c // lap, rows_v.at[0], (rows_sems.at[0], rows_sems.at[1]))
+    kept = []
+
+    def keep(src, dst):
+        copy = pltpu.make_async_copy(src, dst, keep_sems.at[len(kept)])
+        copy.start()
+        kept.append(copy)
+
+    for copy in loads[:weight_loads]:
+        copy.wait()
+    met()
+    main.begin()
+    normed_line.begin()
+    tails.begin()
+
+    pick[...] = head_pick(cw, span, me_c)
+    conv_par[...] = jnp.zeros_like(conv_par)
+    chan_par[...] = jnp.zeros_like(chan_par)
+    for i in range(span):
+        here = pl.ds(i * wide, wide)
+        there = pl.ds(pl.multiple_of(i * apart + wide * me_c, LANES), wide)
+        conv_par[0:CONV_K, here] = conv_w[:, there]
+        conv_par[CONV_K : CONV_K + 1, here] = conv_b[:, there]
+        chan_par[1:2, here] = gate_gain[:, there]
+    conv_par[0:CONV_K, cw:] = conv_w[:, DI:CH]
+    conv_par[CONV_K : CONV_K + 1, cw:] = conv_b[:, DI:CH]
+    picked = dot_exact(heads_in[...], pick[...])
+    heads_par[0:1, :] = picked[0:1, :]
+    heads_par[1:2, :] = -jnp.exp(picked[1:2, :])
+    heads_par[2:8, :] = jnp.zeros((6, LANES), F32)
+    chan_par[0:1, :] = to_lanes(picked[2:3, :], cw)
+    window[...] = jnp.zeros_like(window)
+    state[...] = jnp.zeros_like(state)
+
+    for copy in loads[weight_loads:]:
+        copy.wait()
+    if span == 1:
+        pl.when(held)(rows_load.wait)
+    for d in range(1, nz):
+        normed_line.step(d)
+        if d == 1:
+            cot_line.begin()
+    if nz == 1:
+        cot_line.begin()
+    main.step()
+    tails.step()
+    rows.begin()
+    normed_line.sides()
+
+    def project(depths, first, last):
+        def body(c, _):
+            sums = None
+            for f in depths:
+                a = normed_v[c, :, pl.ds(pl.multiple_of(f * depth, LANES), depth)]
+                both = jnp.concatenate([dot(a, main_v[f]), dot(a, tail_v[f])], axis=1)
+                sums = both if sums is None else sums + both
+            if not first:
+                sums = sums + acc[c]
+            if last:
+                proj[c] = sums.astype(BF16).reshape(proj.shape[1:])
+            else:
+                acc[c] = sums
+            return 0
+
+        lax.fori_loop(0, nc, body, 0)
+
+    if nf == 4:
+        _, fx, fy = square_partners()
+        project([me_f], True, False)
+        project([fx, fy], False, False)
+        keep(normed_v, normed_out)
+        if nz > 1:
+            cot_line.step(1)
+        main.far()
+        tails.far()
+        project([3 - me_f], False, True)
+    else:
+        keep(normed_v, normed_out)
+        for j in range(nf):
+            project([lax.rem(me_f + j, nf)], j == 0, j == nf - 1)
+        if nz > 1:
+            cot_line.step(1)
+    keep(main_v, main_out)
+    keep(tail_v, tail_out)
+    keep(proj, proj_out)
+
+    waiting = [lambda d=d: cot_line.step(d) for d in range(2, nz)]
+    waiting.insert(min(1, len(waiting)), rows.step)
+    for chunk in range(chunks):
+        for s in range(seqs):
+            forward_chunk(
+                cw, chunk, s, lengths, proj, pick, conv_par, heads_par, chan_par, mixed, pre, states,
+                window, state,
+            )
+        if waiting:
+            waiting.pop(0)()
+    while waiting:
+        waiting.pop(0)()
+    keep(mixed, mixed_out)
+    keep(pre, pre_out)
+    keep(states, states_out)
+
+    rows.far()
+    keep(rows_v, rows_out)
+    cot_line.sides()
+    keep(cot_v, cot_out)
+    weights = rows_v[...].reshape(cw, D)
+    for c in range(nc):
+        gg[c] = dot(cot_v[c], weights, 1, 1).reshape(gg.shape[1:])
+    keep(gg, gg_out)
+    ones = jnp.ones((8, cw), F32)
+    across = lambda a: lax.dot_general(
+        ones, a, (((1,), (1,)), ((), ())), precision=EXACT, preferred_element_type=F32
+    )[0:1, :]
+    for chunk in range(chunks):
+        for s in range(seqs):
+            at = pl.ds(chunk * per, per)
+            gate = proj[at, s].reshape(q, proj.shape[3])[:, :cw].astype(F32)
+            g = mixed[chunk, s] * gate * jax.nn.sigmoid(gate)
+            row = 2 * (chunk * seqs + s)
+            stats[row : row + 1, :] = across(g * g)
+            stats[row + 1 : row + 2, :] = across(
+                gg[at, s].reshape(q, cw) * chan_par[1:2, :] * g
+            )
+    exchange = Exchange("ctx", nc, stats, stats_held, (stat_sems.at[0], stat_sems.at[1]))
+    exchange.begin()
+    exchange.wait()
+    totals = exchange.total() * (1.0 / DI)
+    for chunk in range(chunks):
+        for s in range(seqs):
+            row = 2 * (chunk * seqs + s)
+            scale = lax.rsqrt(totals[row : row + 1, :] + EPS)
+            scales[chunk, s, 0:1, :] = scale
+            scales[chunk, s, 1:2, :] = scale * scale * totals[row + 1 : row + 2, :]
+            scales[chunk, s, 2:8, :] = jnp.zeros((6, q), F32)
+    for part in (main, tails, rows, normed_line, cot_line):
+        part.end()
+    for copy in kept:
+        copy.wait()
+
+
+def call_front(nc, nf, cw, span, lengths, hidden, cot, in_w, tail, out_w, norm_gain, conv_w, conv_b, heads_in, gate_gain):
     nz = nc // 2
-    lines = [
-        LineGather(
-            nc, own, every, [line_sems.at[i, j] for j in range(5)] + [here.at[i]]
-        )
-        for i, (own, every) in enumerate(((normed, normed_all), (cot, cot_all)))
+    mine = hidden.shape[0]
+    seqs = lengths.shape[0]
+    length = mine // seqs
+    per = 2 if nc % 2 == 0 else 1
+    q, chunks, cc = per * length, nc // per, cw + 2 * N_STATE
+    depth, wide = in_w.shape[0], cw // span
+    cols = 2 * cw + tail.shape[1]
+    vmem = pl.BlockSpec(memory_space=pltpu.VMEM)
+    anywhere = pl.BlockSpec(memory_space=pl.ANY)
+    dma = pltpu.SemaphoreType.DMA
+    big = [
+        ((nc, mine, D), BF16),
+        ((nc, mine, D), BF16),
+        ((nf, depth, 2 * cw), BF16),
+        ((nf, depth, tail.shape[1]), BF16),
+        ((span, wide, D), BF16),
+        ((nc, seqs, length, cols), BF16),
+        ((nc, seqs, length, cw), F32),
+        ((chunks, seqs, q, cw), F32),
+        ((chunks, seqs, q, cc), F32),
+        ((chunks, seqs, N_STATE, cw), F32),
     ]
-    weights = SquareGather(nf, in_rows, in_all, [in_sems.at[0], in_sems.at[1], here.at[2]])
-    out_args = (out_rows, out_all, [out_sems.at[0], out_sems.at[1], here.at[3]])
-    if spread:
-        outs = Spread(nf, lax.axis_index("ctx") // spread, *out_args)
-    else:
-        outs = SquareGather(nf, *out_args)
-    greet(gather_neighbours(nc, nf))
-    weights.begin()
-    lines[0].begin()
-    for d in range(1, nz):
-        lines[0].step(d)
-        if d == 1:
-            lines[1].begin()
-    weights.step()
-    outs.begin()
-    for d in range(1, nz):
-        lines[1].step(d)
-    if nz == 1:
-        lines[1].begin()
-    outs.step()
-    for part in (weights, lines[0], lines[1], outs):
-        part.end()
-
-
-def call_gather(nc, nf, spread, normed, cot, in_rows, out_rows):
-    every = lambda a, n: jax.ShapeDtypeStruct((n,) + a.shape, a.dtype)
-    nz = nc // 2
+    small = [
+        ((chunks, seqs, 8, q), F32),
+        ((8, cc), F32),
+        ((8, LANES), F32),
+        ((8, cw), F32),
+        ((LANES, LANES), F32),
+    ]
+    held = big[:5] + [((nc, mine, cols), F32)] + big[5:]
+    held += [
+        ((seqs, q + 8, cc), F32),
+        ((seqs, N_STATE, cw), F32),
+        ((2 * chunks * seqs, q), F32),
+        ((nc, 2 * chunks * seqs, q), F32),
+    ]
     places = max(nf, 4)
-    anywhere = pl.BlockSpec(memory_space=pl.ANY)
     return pl.pallas_call(
-        functools.partial(gather_kernel, nc, nf, spread),
-        in_specs=[anywhere] * 4,
-        out_specs=[anywhere] * 4,
-        out_shape=[
-            every(normed, nc),
-            every(cot, nc),
-            every(in_rows, nf),
-            jax.ShapeDtypeStruct(out_rows.shape, BF16) if spread else every(out_rows, nf),
-        ],
-        scratch_shapes=[
-            pltpu.SemaphoreType.DMA((2, 5, nz)),
-            pltpu.SemaphoreType.DMA((2, places)),
-            pltpu.SemaphoreType.DMA((2, places)),
-            pltpu.SemaphoreType.DMA((4,)),
+        functools.partial(front_kernel, nc, nf, cw, span),
+        in_specs=[pl.BlockSpec(memory_space=pltpu.SMEM), vmem, vmem, anywhere, anywhere, anywhere]
+        + [vmem] * 5,
+        out_specs=[anywhere] * len(big) + [vmem] * len(small),
+        out_shape=[jax.ShapeDtypeStruct(*a) for a in big + small],
+        scratch_shapes=[pltpu.VMEM(*a) for a in held]
+        + [
+            dma((2, 5, nz)),
+            dma((2, places)),
+            dma((2, places)),
+            dma((2, places)),
+            dma((2, nc)),
+            dma((2 * span + 3,)),
+            dma((10,)),
         ],
         compiler_params=pltpu.CompilerParams(
             collective_id=0, has_side_effects=True, vmem_limit_bytes=VMEM_LIMIT
         ),
-        name="gather",
-    )(normed, cot, in_rows, out_rows)
-
-
-def add_over_ctx_kernel(nc, own, total, held, send, got):
-    me = lax.axis_index("ctx")
-    peers = [(lax.rem(me + j, nc), lax.rem(me + nc - j, nc)) for j in range(1, nc)]
-    greet([({"ctx": to}, None) for to, _ in peers])
-    for j, (to, _) in enumerate(peers):
-        push(own, held.at[me], send.at[j], got.at[j], {"ctx": to}).start()
-    held[me] = own[...]
-    for j, (to, frm) in enumerate(peers):
-        push(own, held.at[frm], send.at[j], got.at[j], {"ctx": to}).wait()
-    result = held[0]
-    for c in range(1, nc):
-        result = result + held[c]
-    total[...] = result
-
-
-def add_over_ctx(nc, own):
-    return pl.pallas_call(
-        functools.partial(add_over_ctx_kernel, nc),
-        in_specs=[pl.BlockSpec(memory_space=pltpu.VMEM)],
-        out_specs=pl.BlockSpec(memory_space=pltpu.VMEM),
-        out_shape=jax.ShapeDtypeStruct(own.shape, F32),
-        scratch_shapes=[
-            pltpu.VMEM((nc,) + own.shape, F32),
-            pltpu.SemaphoreType.DMA((nc,)),
-            pltpu.SemaphoreType.DMA((nc,)),
-        ],
-        compiler_params=pltpu.CompilerParams(collective_id=1, has_side_effects=True),
-        name="add_over_ctx",
-    )(own)
+        name="front",
+    )(lengths, hidden, cot, in_w, tail, out_w, norm_gain, conv_w, conv_b, heads_in, gate_gain)
 
 
 def add_rows(into, other, rows=16):
@@ -816,35 +947,6 @@
                 out.wait_send()
 
 
-class Exchange:
-    def __init__(self, axis, n, own, every, sems):
-        self.axis, self.n, self.own, self.every = axis, n, own, every
-        self.send, self.got = sems
-
-    def copies(self):
-        me = lax.axis_index(self.axis)
-        for j in range(1, self.n):
-            to, frm = lax.rem(me + j, self.n), lax.rem(me + self.n - j, self.n)
-            args = (self.send.at[j], self.got.at[j], {self.axis: to})
-            yield push(self.own, self.every.at[me], *args), push(self.own, self.every.at[frm], *args)
-
-    def begin(self):
-        self.every[lax.axis_index(self.axis)] = self.own[...]
-        for out, _ in self.copies():
-            out.start()
-
-    def wait(self):
-        for out, arrived in self.copies():
-            arrived.wait_recv()
-            out.wait_send()
-
-    def total(self):
-        result = self.every[0]
-        for i in range(1, self.n):
-            result = result + self.every[i]
-        return result
-
-
 def scatter_kernel(
     nc, nf, strided, dnormed, gin, gout, small, hidden, cot, gain,
     d_hidden, pieces, gout_mine, small_all, gain_all,
@@ -877,7 +979,7 @@
         source = {"ctx": lax.rem(place, nc), "fsdp": place // nc}
         away = lead != place
         found += [(target, away), (source, away)]
-    greet(found)
+    greet(found)()
 
     ins.begin()
     line.begin()
@@ -1042,77 +1144,23 @@
     chunks = nc // per
 
     span = nf if (DI // nf // nc) % LANES == 0 else 1
-    wide, apart = cw // span, DI // span
-    cut = lambda a, start, size, axis: lax.dynamic_slice_in_dim(a, start, size, axis)
-
-    def my_blocks(a, base, axis, unit):
-        return jnp.concatenate(
-            [
-                cut(a, base + (i * apart + wide * me_c) // unit, wide // unit, axis)
-                for i in range(span)
-            ],
-            axis=axis,
-        )
-
+    wide = cw // span
     source = hidden.astype(F32).reshape(seqs, length, D)
-    normed = rms_scale(source, norm_gain).astype(BF16)
     cot = cotangent.reshape(mine, D)
-    in_rows = jnp.concatenate(
-        [
-            my_blocks(input_weight, 0, 1, 1),
-            my_blocks(input_weight, DI, 1, 1),
-            input_weight[:, 2 * DI : 2 * DI + 2 * N_STATE],
-            jnp.pad(
-                my_blocks(input_weight, DI + CH, 1, HEAD_DIM), ((0, 0), (0, LANES - heads))
-            ),
-        ],
-        axis=1,
-    )
-    shard = output_weight.shape[0]
-    if span > 1:
-        out_rows = cut(output_weight, wide * me_c, wide, 0)
-        spread = 0
-    else:
-        spread = shard // cw
-        out_rows = cut(output_weight, cw * lax.rem(me_c, spread), cw, 0)
-    normed_all, cot_all, in_w, out_w = call_gather(
-        nc, nf, spread, normed.reshape(mine, D), cot, in_rows, out_rows
+    tail = input_weight[:, 2 * DI :]
+    tail = jnp.pad(tail, ((0, 0), (0, -tail.shape[1] % LANES)))
+    heads_in = jnp.pad(jnp.stack([dt_bias, a_log, d_skip]), ((0, 5), (0, LANES - HEADS)))
+    seq_lengths = lengths.reshape(seqs)
+    (
+        normed_all, cot_all, main_w, tail_w, out_w, proj, grad_gated, mixed, pre, states,
+        scales, conv_par, heads_par, chan_par, pick,
+    ) = call_front(
+        nc, nf, cw, span, seq_lengths, hidden.reshape(mine, D), cot, input_weight, tail, output_weight,
+        norm_gain[None], conv_w, conv_b[None], heads_in, gate_gain[None],
     )
     normed_all, cot_all = normed_all.reshape(nc * mine, D), cot_all.reshape(nc * mine, D)
-    in_w, out_w = in_w.reshape(D, -1), out_w.reshape(cw, D)
-
-    my_columns = lambda a: jnp.concatenate(
-        [my_blocks(a, 0, 1, 1), lax.slice_in_dim(a, DI, CH, axis=1)], axis=1
-    )
-    conv_par = jnp.concatenate(
-        [my_columns(conv_w), my_columns(conv_b[None]), jnp.zeros((3, cc), F32)], axis=0
-    )
-    per_head = lambda a: my_blocks(a, 0, 0, HEAD_DIM)
-    pad_heads = lambda a: jnp.pad(a, (0, LANES - heads))[None]
-    rate = -jnp.exp(per_head(a_log))
-    heads_par = jnp.concatenate(
-        [pad_heads(per_head(dt_bias)), pad_heads(rate), jnp.zeros((6, LANES), F32)], axis=0
-    )
-    chan_par = jnp.concatenate(
-        [
-            jnp.repeat(per_head(d_skip), HEAD_DIM)[None],
-            my_blocks(gate_gain, 0, 0, 1)[None],
-            jnp.zeros((6, cw), F32),
-        ],
-        axis=0,
-    )
-    seq_lengths = lengths.reshape(seqs)
-
-    proj = dot(normed_all, in_w).astype(BF16).reshape(nc, seqs, length, -1)
-    grad_gated = dot(cot_all, out_w, 1, 1).reshape(nc, seqs, length, cw)
-    mixed, pre, states, stats = call_forward(
-        cw, per, seq_lengths, proj, conv_par, heads_par, chan_par, grad_gated
-    )
-    totals = add_over_ctx(nc, stats[:, :, 0:2].reshape(chunks * seqs * 2, q)) / DI
-    totals = totals.reshape(chunks, seqs, 2, q)
-    scale = lax.rsqrt(totals[:, :, 0] + EPS)
-    pull = scale * scale * totals[:, :, 1]
-    scales = jnp.pad(jnp.stack([scale, pull], axis=2), ((0, 0), (0, 0), (0, 6), (0, 0)))
+    out_w = out_w.reshape(cw, D)
+    scale = scales[:, :, 0]
 
     by_chunk = lambda a: jnp.moveaxis(
         a.reshape(chunks, seqs, per, length, a.shape[-1]), 2, 1
@@ -1125,11 +1173,13 @@
     out = lax.psum_scatter(branch, "ctx", scatter_dimension=0).astype(F32) + source.reshape(mine, D)
 
     dproj, dconv, dheads, dchan = call_backward(
-        cw, per, seq_lengths, proj, conv_par, heads_par, chan_par, grad_gated, mixed, pre, states,
-        scales,
+        cw, per, seq_lengths, proj, pick, conv_par, heads_par, chan_par, grad_gated, mixed, pre,
+        states, scales,
     )
     dproj = dproj.reshape(nc * mine, -1)
-    dnormed = dot(dproj, in_w, 1, 1).astype(BF16).reshape(nc, mine, D)
+    dnormed = dot(dproj[:, : 2 * cw], main_w.reshape(D, -1), 1, 1)
+    dnormed = dnormed + dot(dproj[:, 2 * cw :], tail_w.reshape(D, -1), 1, 1)
+    dnormed = dnormed.astype(BF16).reshape(nc, mine, D)
     rows = D // (nc * nf)
     gin = dot(normed_all, dproj, 0, 0).astype(BF16).reshape(nc, nf, rows, -1)
     gin = jnp.swapaxes(gin, 0, 1)
@@ -1155,8 +1205,9 @@
         [
             ordered(pieces[:, :, :cw]),
             ordered(pieces[:, :, cw : 2 * cw]),
-            jnp.sum(pieces[:, :, 2 * cw : 2 * cw + 2 * N_STATE].astype(F32), axis=0).astype(BF16),
-            ordered(pieces[:, :, 2 * cw + 2 * N_STATE : 2 * cw + 2 * N_STATE + heads]),
+            jnp.sum(pieces[:, :, 2 * cw : 2 * cw + 2 * N_STATE + HEADS].astype(F32), axis=0).astype(
+                BF16
+            ),
         ],
         axis=1,
     ).astype(F32)

time: 400 us -> 364 us (0.910)
  the two profiles are of different devices: /device:TPU:1 before, /device:TPU:28 now
where the time goes in v4:
time: 364 us; the launch traced here: 360 us
  Pallas kernels  271 us (74%)
  local copies, waits for them, and re-layouts  36.4 us (10%)
  matrix products  26.9 us (7%)
  between operations  14.5 us (4%)
  other arithmetic  11.8 us (3%)
    pallas_call x1, Pallas kernels, call_scatter(): pl.pallas_call(functools.partial(scatter_kernel, nc, nf, strided), in_spe...  143 us
    pallas_call x1, Pallas kernels, call_front(): pl.pallas_call(functools.partial(front_kernel, nc, nf, cw, span), in_spec...  100 us
    pallas_call x1, Pallas kernels, call_backward(): pl.pallas_call(functools.partial(backward_kernel, cw, chunks), grid=(chun...  27.4 us
    dot_general x5, matrix products, dot(): lax.dot_general(a.astype(BF16), b.astype(BF16), (((ca,), (cb,)), ((), ())...  26.9 us
    unnamed x30, local copies, waits for them, and re-layouts  14.1 us
  transfers between devices with their start and end apart: 1, of which 0 were waited for; matrix products, arithmetic and copies ran while one was open for 13% of the time, Pallas kernels for 47%

profile of v4, /device:TPU:28, one launch (start us, length us, event | category | flops | bytes accessed | tf_op | source)
XLA Modules:
  0.0 360.2 jit_solution(11654647946412605465)
XLA Ops:
  7.3 12.3 %copy.64.in_w = bf16[512,8512]{1,0:T(8,128)(2,1)} copy(bf16[512,8512]{0,1:T(8,128)(2,1)} %param.16) | data formatting | bytes 17432576 | tf_op args[4]
  19.6 1.0 slice.103
  22.7 100.4 %front.1 = (bf16[8,128,2048]{2,1,0:T(8,128)(2,1)}, bf16[8,128,2048]{2,1,0:T(8,128)(2,1)}, bf16[4,512,1024]{2,1,0:T(8,128)(2,1)}, bf16[4,512,384]{2,1,0:T(8,128)(...) custom-call(s32[2]{0:T(128)} %bitcast.107, ...), custom_call_target="tpu_custom_call" | custom-call | tf_op jit(solution)/shard_map/front/pallas_call | solution.py:763
  123.0 1.8 fusion.11
  126.6 2.1 fusion.8
  128.8 4.4 %convolution_convert_fusion.1 = bf16[1024,2048]{1,0:T(8,128)(2,1)} fusion(bf16[1024,512]{1,0:T(8,128)(2,1)S(1)} %bitcast.92, bf16[512,2048]{1,0:T(8,128)(2,1)S(1)} %bitcast.115), kind=kOutput, calls=%fused_computation.3 | convolution fusion | flops 2149580800 | bytes 7340032 | tf_op jit(solution)/shard_map/dot_general | solution.py:26
  133.1 27.4 %mixer_backward.1 = (bf16[8,2,64,1408]{3,2,1,0:T(8,128)(2,1)}, f32[8,768]{1,0:T(8,128)}, f32[8,128]{1,0:T(8,128)}, f32[8,512]{1,0:T(8,128)}) custom-call(s32[2]{0:T(128)} %bitcast.108, bf16[8,2,64,1408]{3,2,1,0:T(8,128)(2,1)} %get-tuple-element.38.proj, f32[128,128]{1,0:T(8,128)} %get-tuple-element.43.pick, f32[8,768]{1,0:T(8,128)} %get-tuple-element.44.conv_w, ...), custom_call_target="tpu_custom_call" | custom-call | tf_op jit(solution)/shard_map/mixer_backward/pallas_call | solution.py:255
  163.4 9.9 %convolution_convert_fusion = bf16[2048,1408]{1,0:T(8,128)(2,1)S(1)} fusion(bf16[1024,2048]{1,0:T(8,128)(2,1)} %bitcast.114, bf16[1024,1408]{1,0:T(8,128)(2,1)} %bitcast.96), kind=kOutput, calls=%fused_computation.1 | convolution fusion | flops 5908463616 | bytes 12845056 | tf_op jit(solution)/shard_map/dot_general | solution.py:26
  173.2 3.4 copy.88
  177.3 3.7 %convolution_convert_fusion.2 = bf16[512,2048]{1,0:T(8,128)(2,1)} fusion(bf16[1024,512]{1,0:T(8,128)(2,1)S(1)} %bitcast.93, bf16[1024,2048]{1,0:T(8,128)(2,1)S(1)} %bitcast.113), kind=kOutput, calls=%fused_computation.4 | convolution fusion | flops 2148532224 | bytes 7340032 | tf_op jit(solution)/shard_map/dot_general | solution.py:26
  181.0 4.5 %fusion.6 = f32[1024,2048]{1,0:T(8,128)S(1)} fusion(bf16[2048,1024]{1,0:T(8,128)(2,1)S(1)} %bitcast.112, bf16[1024,1408]{1,0:T(8,128)(2,1)S(1)} %bitcast.97), kind=kOutput, calls=%fused_computation.13 | convolution fusion | flops 4294967296 | bytes 14680064 | tf_op jit(solution)/shard_map/dot_general | solution.py:26
  185.5 4.5 %add_convert_fusion = bf16[1024,2048]{1,0:T(8,128)(2,1)} fusion(f32[1024,2048]{1,0:T(8,128)S(1)} %fusion.6, bf16[2048,384]{1,0:T(8,128)(2,1)S(1)} %bitcast.90, bf16[1024,1408]{1,0:T(8,128)(2,1)S(1)} %bitcast.98), kind=kOutput, calls=%fused_computation | convolution fusion | flops 1614807040 | bytes 14942208 | tf_op jit(solution)/shard_map/dot_general | solution.py:26
  190.6 142.9 %scatter.1 = (f32[128,2048]{1,0:T(8,128)}, bf16[8,64,1408]{2,1,0:T(8,128)(2,1)}, bf16[2,64,2048]{2,1,0:T(8,128)(2,1)}, f32[8,40,128]{2,1,0:T(8,128)}, f32[8,8,2048]{2,1,0:T(8,128)}) custom-call(bf16[8,128,2048]{2,1,0:T(8,128)(2,1)} %bitcast.77, bf16[4,8,64,1408]{3,2,1,0:T(8,128)(2,1)} %bitcast.76, bf16[4,2,64,2048]{3,2,1,0:T(8,128)(2,1)} %bitcast.89, ...), custom_call_target="tpu_custom_call" | custom-call | tf_op jit(solution)/shard_map/scatter/pallas_call | solution.py:1077
  333.6 0.9 slice.94
  334.5 0.8 slice.100
  335.3 0.9 slice_reduce_fusion.1
  336.9 1.3 fusion.12
  341.4 0.8 fusion.13
  344.5 1.7 slice_reduce_fusion.2
  346.2 1.1 slice_reduce_fusion
  347.2 1.1 bitcast_convert_fusion
  348.8 1.5 maximum_convert_fusion
  350.3 2.0 fusion.9
  352.2 1.0 copy.92
  (72 shorter events, 14.5 us)
Async XLA Ops:
  7.2 13.5 %copy-start.6 = (f32[4352]{0:T(1024)S(1)}, f32[4352]{0:T(1024)}, u32[]{:S(2)}) copy-start(f32[4352]{0:T(1024)} %param.18) | copy-start | bytes 52228
  7.2 14.9 %copy-start.9 = (f32[64]{0:T(128)S(1)}, f32[64]{0:T(128)}, u32[]{:S(2)}) copy-start(f32[64]{0:T(128)} %param.19) | copy-start | bytes 772
  7.2 14.9 %copy-start.8 = (f32[64]{0:T(128)S(1)}, f32[64]{0:T(128)}, u32[]{:S(2)}) copy-start(f32[64]{0:T(128)} %param.20) | copy-start | bytes 772
  7.2 14.9 %copy-start.7 = (f32[64]{0:T(128)S(1)}, f32[64]{0:T(128)}, u32[]{:S(2)}) copy-start(f32[64]{0:T(128)} %param.21) | copy-start | bytes 772
  7.2 343.0 %reduce-scatter.2.cloned.1.call-start = ((), (), s32[]{:S(2)}) async-start(), calls=%async_computation.1 | async-start | bytes 4718592 | tf_op jit(solution)/shard_map/reduce_scatter | solution.py:1173
  126.6 2.1 copy-start.12
  173.2 4.0 %copy-start.11 = (bf16[8,128,2048]{2,1,0:T(8,128)(2,1)S(1)}, bf16[8,128,2048]{2,1,0:T(8,128)(2,1)}, u32[]{:S(2)}) copy-start(bf16[8,128,2048]{2,1,0:T(8,128)(2,1)} %get-tuple-element.54) | copy-start | bytes 12582916
  177.3 3.7 %copy-start.4 = (bf16[8,2,64,1408]{3,2,1,0:T(8,128)(2,1)S(1)}, bf16[8,2,64,1408]{3,2,1,0:T(8,128)(2,1)}, u32[]{:S(2)}) copy-start(bf16[8,2,64,1408]{3,2,1,0:T(8,128)(2,1)} %get-tuple-element.50) | copy-start | bytes 8650756
  177.3 3.7 %copy-start.10 = (bf16[4,512,1024]{2,1,0:T(8,128)(2,1)S(1)}, bf16[4,512,1024]{2,1,0:T(8,128)(2,1)}, u32[]{:S(2)}) copy-start(bf16[4,512,1024]{2,1,0:T(8,128)(2,1)} %get-tuple-element.51) | copy-start | bytes 12582916
  181.0 4.5 %copy-start.1 = (bf16[4,512,384]{2,1,0:T(8,128)(2,1)S(1)}, bf16[4,512,384]{2,1,0:T(8,128)(2,1)}, u32[]{:S(2)}) copy-start(bf16[4,512,384]{2,1,0:T(8,128)(2,1)} %get-tuple-element.52) | copy-start | bytes 4718596
  185.5 4.5 %copy-start.5 = (f32[2048]{0:T(1024)S(1)}, f32[2048]{0:T(1024)}, u32[]{:S(2)}) copy-start(f32[2048]{0:T(1024)} %param.15) | copy-start | bytes 24580
  338.4 8.9 %copy-start.3 = (bf16[2,64,2048]{2,1,0:T(8,128)(2,1)S(1)}, bf16[2,64,2048]{2,1,0:T(8,128)(2,1)}, u32[]{:S(2)}) copy-start(bf16[2,64,2048]{2,1,0:T(8,128)(2,1)} %get-tuple-element.62) | copy-start | bytes 1572868
  348.3 1.9 copy-start
  348.7 3.5 copy-start.2
Sparse Core Ops, SparseCore 0:
  133.3 47.6 reduce-scatter.1
